TPU v7x, 256 devices: a whole 4x4x8 slice. The times are simulated.
256 devices in a mesh: panel: 16 (over z_hi, y, core), front: 16 (over z_lo, x).
Axes of the slice: x: 4, y: 4, z: 8 (z_hi: 2, z_lo: 4; z = z_hi * 4 + z_lo), core: 2. Of those that a mesh axis runs over, the one named last changes fastest.
Arguments:
- source_leaf: float32 [16, 32, 32, 1024], P('panel', 'front'), may hold values from -6 to 6
- source_sep: float32 [16, 32, 4096], P('panel', None, 'front'), may hold values from -6 to 6
- leaf_inverse: bfloat16 [16, 32, 1024, 1024], P('panel', 'front'), as said below
- lift: bfloat16 [16, 32, 1024, 512], P('panel', 'front'), may hold values from -0.1875 to 0.1875
- lower: bfloat16 [16, 32, 512, 1024], P('panel', 'front'), may hold values from -0.25 to 0.25
- sep_inverse: bfloat16 [16, 4096, 4096], P('panel', None, 'front'), as said below
- parent_map: int32 [16, 32, 512], P('panel', 'front'), may hold values from 0 to 4095, as said below
- couple_down: float32 [16, 32, 1024], P('panel', 'front'), may hold values from 0.6 to 1.2
- couple_up: float32 [16, 32, 1024], P('panel', 'front'), may hold values from 0.6 to 1.2
Outputs:
- leaf_solution: float32 [16, 32, 32, 1024], P('panel', 'front')
- sep_solution: float32 [16, 32, 4096], P('panel', None, 'front')
Inputs may be any that keep to these rules, and one draw needn't show every extreme that they name: `leaf_inverse`: each leaf inverse factor is dense; its diagonal entries lie near 0.8 to 1.1, and its off-diagonal part is not small in sum. `sep_inverse`: each separator inverse factor is dense; its diagonal entries lie near 0.8 to 1.1, and its off-diagonal part is not small in sum. `parent_map`: within one front the 512 entries are distinct; update rows o * 32 to (o + 1) * 32 - 1 of every front name only unknowns o * 256 to (o + 1) * 256 - 1; every separator unknown of a panel is named by exactly 4 fronts.
All inputs are finite; a program needn't handle non-finite values.
Results may differ from a plain program's by a relative error of at most 0.02.
Values may be sent and summed in bfloat16 or wider, within the bound.
A program may use at most 64 MiB of HBM per device.

v0:
```python
import jax
import jax.numpy as jnp
from jax import lax
from jax.sharding import PartitionSpec as P


def shifted(block, axis, distance):
    devices = range(lax.axis_size(axis))
    route = [(i - distance, i) for i in devices if i - distance in devices]
    return lax.ppermute(block, axis, route)


def leaf_apply(loaded, inverse):
    return jnp.einsum(
        "fbl,flm->fbm", loaded.astype(jnp.bfloat16), inverse, preferred_element_type=jnp.float32
    )


def local(
    source_leaf,
    source_sep,
    leaf_inverse,
    lift,
    lower,
    sep_inverse,
    parent_map,
    couple_down,
    couple_up,
):
    source = source_leaf[0]
    inverse = leaf_inverse[0]
    down_coupling = couple_down[0][:, None, :]
    up_coupling = couple_up[0][:, None, :]
    parents = parent_map[0]
    panels = lax.axis_size("panel")
    position = lax.axis_index("panel")
    groups = 1
    block_rows = source.shape[1] // groups
    rounds = panels + groups - 1
    zero_trace = jnp.zeros((source.shape[0], block_rows, source.shape[2]), jnp.bfloat16)

    def down_step(step, carry):
        trace, stored = carry
        group = step - position
        valid = jnp.logical_and(group >= 0, group < groups)
        loaded = source + down_coupling * trace.astype(jnp.float32)
        solved = leaf_apply(loaded, inverse)
        before = stored
        stored = jnp.where(valid, loaded, before)
        trace = shifted(solved.astype(jnp.bfloat16), "panel", 1)
        return (trace, stored)

    _, stored = lax.fori_loop(0, rounds, down_step, (zero_trace, jnp.zeros_like(source)))

    def up_step(step, carry):
        trace, swept = carry
        group = step - (panels - 1 - position)
        valid = jnp.logical_and(group >= 0, group < groups)
        loaded = stored + up_coupling * trace.astype(jnp.float32)
        solved = leaf_apply(loaded, inverse)
        before = swept
        swept = jnp.where(valid, solved, before)
        trace = shifted(solved.astype(jnp.bfloat16), "panel", -1)
        return (trace, swept)

    _, swept = lax.fori_loop(0, rounds, up_step, (zero_trace, jnp.zeros_like(source)))
    total_rows = source.shape[1]
    sep_total = sep_inverse.shape[1]
    swept_half = swept.astype(jnp.bfloat16)
    update = jnp.einsum("fbl,flu->fbu", swept_half, lift[0], preferred_element_type=jnp.float32)
    flat = jnp.transpose(update, (1, 0, 2)).reshape(total_rows, -1)
    placed = jnp.zeros((total_rows, sep_total), jnp.float32).at[:, parents.reshape(-1)].add(flat)
    gathered = lax.psum_scatter(placed, "front", scatter_dimension=1, tiled=True)
    reduced = (source_sep[0] - gathered).astype(jnp.bfloat16)
    sep_rows = sep_inverse[0]
    sep_solved = jnp.dot(
        lax.all_gather(reduced, "front", axis=1, tiled=True),
        sep_rows,
        preferred_element_type=jnp.float32,
    )
    whole_sep = lax.all_gather(sep_solved.astype(jnp.bfloat16), "front", axis=1, tiled=True)
    picked = whole_sep[:, parents]
    back = jnp.einsum("bfu,ful->fbl", picked, lower[0], preferred_element_type=jnp.float32)
    leaf_solution = swept - back
    return (leaf_solution[None], sep_solved[None])


def solution(mesh):
    return jax.shard_map(
        local,
        mesh=mesh,
        in_specs=(
            P("panel", "front", None, None),
            P("panel", None, "front"),
            P("panel", "front", None, None),
            P("panel", "front", None, None),
            P("panel", "front", None, None),
            P("panel", None, "front"),
            P("panel", "front", None),
            P("panel", "front", None),
            P("panel", "front", None),
        ),
        out_specs=(P("panel", "front", None, None), P("panel", None, "front")),
        check_vma=False,
    )
```

profile of v0, /device:TPU:8, one launch (start us, length us, event | category | flops | bytes accessed | tf_op | source)
XLA Modules:
  0.0 697.7 jit_solution(346078378654525253)
XLA Ops:
  7.3 204.7 %while.34 = (s32[]{:T(128)}, bf16[2,32,1024]{2,1,0:T(8,128)(2,1)S(1)}, f32[2,32,1024]{2,1,0:T(8,128)S(1)}, f32[2,1,1024]{2,0,1:T(2,128)}, f32[2,32,1024]{2,1,0:T...) while((s32[]{:T(128)}, bf16[2,32,1024]{2,1,0:T(8,128)(2,1)S(1)}, ...), condition=%wide.region_1.2_spmd.clone, body=%wide.region_0.1_spmd.clone.sunk | while | flops 134873088 | bytes 7520489 | solution.py:53
  77.0 10.0 %collective-permute-start = (bf16[2,32,1024]{2,1,0:T(8,128)(2,1)S(1)}, bf16[2,32,1024]{2,1,0:T(8,128)(2,1)S(1)}, u32[]{:S(2)}, u32[]{:S(2)}) collective-permute-start(bf16[2,32,1024]{2,1,0:T(8,128)(2,1)S(1)} %convolution_convert_fusion.2), channel_id=1, source_target_pairs={{0,16},{16,32},{32,48},{48,64},{64,80},{80,96},{96,112},{112,128},... | collective-permute-start | bytes 393224 | tf_op jit(solution)/shard_map/while/body/eval_jaxpr/ppermute | solution.py:10
  91.2 11.3 %collective-permute-start = (bf16[2,32,1024]{2,1,0:T(8,128)(2,1)S(1)}, bf16[2,32,1024]{2,1,0:T(8,128)(2,1)S(1)}, u32[]{:S(2)}, u32[]{:S(2)}) collective-permute-start(bf16[2,32,1024]{2,1,0:T(8,128)(2,1)S(1)} %convolution_convert_fusion.2), channel_id=1, source_target_pairs={{0,16},{16,32},{32,48},{48,64},{64,80},{80,96},{96,112},{112,128},... | collective-permute-start | bytes 393224 | tf_op jit(solution)/shard_map/while/body/eval_jaxpr/ppermute | solution.py:10
  106.7 11.3 %collective-permute-start = (bf16[2,32,1024]{2,1,0:T(8,128)(2,1)S(1)}, bf16[2,32,1024]{2,1,0:T(8,128)(2,1)S(1)}, u32[]{:S(2)}, u32[]{:S(2)}) collective-permute-start(bf16[2,32,1024]{2,1,0:T(8,128)(2,1)S(1)} %convolution_convert_fusion.2), channel_id=1, source_target_pairs={{0,16},{16,32},{32,48},{48,64},{64,80},{80,96},{96,112},{112,128},... | collective-permute-start | bytes 393224 | tf_op jit(solution)/shard_map/while/body/eval_jaxpr/ppermute | solution.py:10
  122.2 11.3 %collective-permute-start = (bf16[2,32,1024]{2,1,0:T(8,128)(2,1)S(1)}, bf16[2,32,1024]{2,1,0:T(8,128)(2,1)S(1)}, u32[]{:S(2)}, u32[]{:S(2)}) collective-permute-start(bf16[2,32,1024]{2,1,0:T(8,128)(2,1)S(1)} %convolution_convert_fusion.2), channel_id=1, source_target_pairs={{0,16},{16,32},{32,48},{48,64},{64,80},{80,96},{96,112},{112,128},... | collective-permute-start | bytes 393224 | tf_op jit(solution)/shard_map/while/body/eval_jaxpr/ppermute | solution.py:10
  137.7 11.3 %collective-permute-start = (bf16[2,32,1024]{2,1,0:T(8,128)(2,1)S(1)}, bf16[2,32,1024]{2,1,0:T(8,128)(2,1)S(1)}, u32[]{:S(2)}, u32[]{:S(2)}) collective-permute-start(bf16[2,32,1024]{2,1,0:T(8,128)(2,1)S(1)} %convolution_convert_fusion.2), channel_id=1, source_target_pairs={{0,16},{16,32},{32,48},{48,64},{64,80},{80,96},{96,112},{112,128},... | collective-permute-start | bytes 393224 | tf_op jit(solution)/shard_map/while/body/eval_jaxpr/ppermute | solution.py:10
  153.2 11.3 %collective-permute-start = (bf16[2,32,1024]{2,1,0:T(8,128)(2,1)S(1)}, bf16[2,32,1024]{2,1,0:T(8,128)(2,1)S(1)}, u32[]{:S(2)}, u32[]{:S(2)}) collective-permute-start(bf16[2,32,1024]{2,1,0:T(8,128)(2,1)S(1)} %convolution_convert_fusion.2), channel_id=1, source_target_pairs={{0,16},{16,32},{32,48},{48,64},{64,80},{80,96},{96,112},{112,128},... | collective-permute-start | bytes 393224 | tf_op jit(solution)/shard_map/while/body/eval_jaxpr/ppermute | solution.py:10
  168.7 11.3 %collective-permute-start = (bf16[2,32,1024]{2,1,0:T(8,128)(2,1)S(1)}, bf16[2,32,1024]{2,1,0:T(8,128)(2,1)S(1)}, u32[]{:S(2)}, u32[]{:S(2)}) collective-permute-start(bf16[2,32,1024]{2,1,0:T(8,128)(2,1)S(1)} %convolution_convert_fusion.2), channel_id=1, source_target_pairs={{0,16},{16,32},{32,48},{48,64},{64,80},{80,96},{96,112},{112,128},... | collective-permute-start | bytes 393224 | tf_op jit(solution)/shard_map/while/body/eval_jaxpr/ppermute | solution.py:10
  184.2 11.3 %collective-permute-start = (bf16[2,32,1024]{2,1,0:T(8,128)(2,1)S(1)}, bf16[2,32,1024]{2,1,0:T(8,128)(2,1)S(1)}, u32[]{:S(2)}, u32[]{:S(2)}) collective-permute-start(bf16[2,32,1024]{2,1,0:T(8,128)(2,1)S(1)} %convolution_convert_fusion.2), channel_id=1, source_target_pairs={{0,16},{16,32},{32,48},{48,64},{64,80},{80,96},{96,112},{112,128},... | collective-permute-start | bytes 393224 | tf_op jit(solution)/shard_map/while/body/eval_jaxpr/ppermute | solution.py:10
  199.7 11.3 %collective-permute-start = (bf16[2,32,1024]{2,1,0:T(8,128)(2,1)S(1)}, bf16[2,32,1024]{2,1,0:T(8,128)(2,1)S(1)}, u32[]{:S(2)}, u32[]{:S(2)}) collective-permute-start(bf16[2,32,1024]{2,1,0:T(8,128)(2,1)S(1)} %convolution_convert_fusion.2), channel_id=1, source_target_pairs={{0,16},{16,32},{32,48},{48,64},{64,80},{80,96},{96,112},{112,128},... | collective-permute-start | bytes 393224 | tf_op jit(solution)/shard_map/while/body/eval_jaxpr/ppermute | solution.py:10
  212.1 247.2 %while.35 = (s32[]{:T(128)}, bf16[2,32,1024]{2,1,0:T(8,128)(2,1)S(1)}, f32[2,32,1024]{2,1,0:T(8,128)S(1)}, f32[2,1,1024]{2,0,1:T(2,128)S(1)}, f32[2,32,1024]{2,1...) while((s32[]{:T(128)}, ...), condition=%wide.region_3.4_spmd.clone, body=%wide.region_2.3_spmd.clone.sunk | while | flops 134676480 | bytes 5775537 | solution.py:66
  217.1 10.2 %collective-permute-done.1 = bf16[2,32,1024]{2,1,0:T(8,128)(2,1)S(1)} collective-permute-done((bf16[2,32,1024]{2,1,0:T(8,128)(2,1)S(1)}, bf16[2,32,1024]{2,1,0:T(8,128)(2,1)S(1)}, u32[]{:S(2)}, u32[]{:S(2)}) %collective-permute-start.1) | collective-permute-done | bytes 131104 | tf_op jit(solution)/shard_map/while/body/eval_jaxpr/ppermute | solution.py:10
  232.3 11.1 %collective-permute-done.1 = bf16[2,32,1024]{2,1,0:T(8,128)(2,1)S(1)} collective-permute-done((bf16[2,32,1024]{2,1,0:T(8,128)(2,1)S(1)}, bf16[2,32,1024]{2,1,0:T(8,128)(2,1)S(1)}, u32[]{:S(2)}, u32[]{:S(2)}) %collective-permute-start.1) | collective-permute-done | bytes 131104 | tf_op jit(solution)/shard_map/while/body/eval_jaxpr/ppermute | solution.py:10
  248.3 10.2 %collective-permute-done.1 = bf16[2,32,1024]{2,1,0:T(8,128)(2,1)S(1)} collective-permute-done((bf16[2,32,1024]{2,1,0:T(8,128)(2,1)S(1)}, bf16[2,32,1024]{2,1,0:T(8,128)(2,1)S(1)}, u32[]{:S(2)}, u32[]{:S(2)}) %collective-permute-start.1) | collective-permute-done | bytes 131104 | tf_op jit(solution)/shard_map/while/body/eval_jaxpr/ppermute | solution.py:10
  263.5 11.1 %collective-permute-done.1 = bf16[2,32,1024]{2,1,0:T(8,128)(2,1)S(1)} collective-permute-done((bf16[2,32,1024]{2,1,0:T(8,128)(2,1)S(1)}, bf16[2,32,1024]{2,1,0:T(8,128)(2,1)S(1)}, u32[]{:S(2)}, u32[]{:S(2)}) %collective-permute-start.1) | collective-permute-done | bytes 131104 | tf_op jit(solution)/shard_map/while/body/eval_jaxpr/ppermute | solution.py:10
  279.6 10.2 %collective-permute-done.1 = bf16[2,32,1024]{2,1,0:T(8,128)(2,1)S(1)} collective-permute-done((bf16[2,32,1024]{2,1,0:T(8,128)(2,1)S(1)}, bf16[2,32,1024]{2,1,0:T(8,128)(2,1)S(1)}, u32[]{:S(2)}, u32[]{:S(2)}) %collective-permute-start.1) | collective-permute-done | bytes 131104 | tf_op jit(solution)/shard_map/while/body/eval_jaxpr/ppermute | solution.py:10
  294.8 11.1 %collective-permute-done.1 = bf16[2,32,1024]{2,1,0:T(8,128)(2,1)S(1)} collective-permute-done((bf16[2,32,1024]{2,1,0:T(8,128)(2,1)S(1)}, bf16[2,32,1024]{2,1,0:T(8,128)(2,1)S(1)}, u32[]{:S(2)}, u32[]{:S(2)}) %collective-permute-start.1) | collective-permute-done | bytes 131104 | tf_op jit(solution)/shard_map/while/body/eval_jaxpr/ppermute | solution.py:10
  310.8 10.4 %collective-permute-done.1 = bf16[2,32,1024]{2,1,0:T(8,128)(2,1)S(1)} collective-permute-done((bf16[2,32,1024]{2,1,0:T(8,128)(2,1)S(1)}, bf16[2,32,1024]{2,1,0:T(8,128)(2,1)S(1)}, u32[]{:S(2)}, u32[]{:S(2)}) %collective-permute-start.1) | collective-permute-done | bytes 131104 | tf_op jit(solution)/shard_map/while/body/eval_jaxpr/ppermute | solution.py:10
  326.2 10.4 %collective-permute-done.1 = bf16[2,32,1024]{2,1,0:T(8,128)(2,1)S(1)} collective-permute-done((bf16[2,32,1024]{2,1,0:T(8,128)(2,1)S(1)}, bf16[2,32,1024]{2,1,0:T(8,128)(2,1)S(1)}, u32[]{:S(2)}, u32[]{:S(2)}) %collective-permute-start.1) | collective-permute-done | bytes 131104 | tf_op jit(solution)/shard_map/while/body/eval_jaxpr/ppermute | solution.py:10
  341.5 10.4 %collective-permute-done.1 = bf16[2,32,1024]{2,1,0:T(8,128)(2,1)S(1)} collective-permute-done((bf16[2,32,1024]{2,1,0:T(8,128)(2,1)S(1)}, bf16[2,32,1024]{2,1,0:T(8,128)(2,1)S(1)}, u32[]{:S(2)}, u32[]{:S(2)}) %collective-permute-start.1) | collective-permute-done | bytes 131104 | tf_op jit(solution)/shard_map/while/body/eval_jaxpr/ppermute | solution.py:10
  356.8 10.4 %collective-permute-done.1 = bf16[2,32,1024]{2,1,0:T(8,128)(2,1)S(1)} collective-permute-done((bf16[2,32,1024]{2,1,0:T(8,128)(2,1)S(1)}, bf16[2,32,1024]{2,1,0:T(8,128)(2,1)S(1)}, u32[]{:S(2)}, u32[]{:S(2)}) %collective-permute-start.1) | collective-permute-done | bytes 131104 | tf_op jit(solution)/shard_map/while/body/eval_jaxpr/ppermute | solution.py:10
  372.2 10.4 %collective-permute-done.1 = bf16[2,32,1024]{2,1,0:T(8,128)(2,1)S(1)} collective-permute-done((bf16[2,32,1024]{2,1,0:T(8,128)(2,1)S(1)}, bf16[2,32,1024]{2,1,0:T(8,128)(2,1)S(1)}, u32[]{:S(2)}, u32[]{:S(2)}) %collective-permute-start.1) | collective-permute-done | bytes 131104 | tf_op jit(solution)/shard_map/while/body/eval_jaxpr/ppermute | solution.py:10
  387.5 10.4 %collective-permute-done.1 = bf16[2,32,1024]{2,1,0:T(8,128)(2,1)S(1)} collective-permute-done((bf16[2,32,1024]{2,1,0:T(8,128)(2,1)S(1)}, bf16[2,32,1024]{2,1,0:T(8,128)(2,1)S(1)}, u32[]{:S(2)}, u32[]{:S(2)}) %collective-permute-start.1) | collective-permute-done | bytes 131104 | tf_op jit(solution)/shard_map/while/body/eval_jaxpr/ppermute | solution.py:10
  402.8 10.4 %collective-permute-done.1 = bf16[2,32,1024]{2,1,0:T(8,128)(2,1)S(1)} collective-permute-done((bf16[2,32,1024]{2,1,0:T(8,128)(2,1)S(1)}, bf16[2,32,1024]{2,1,0:T(8,128)(2,1)S(1)}, u32[]{:S(2)}, u32[]{:S(2)}) %collective-permute-start.1) | collective-permute-done | bytes 131104 | tf_op jit(solution)/shard_map/while/body/eval_jaxpr/ppermute | solution.py:10
  418.2 10.4 %collective-permute-done.1 = bf16[2,32,1024]{2,1,0:T(8,128)(2,1)S(1)} collective-permute-done((bf16[2,32,1024]{2,1,0:T(8,128)(2,1)S(1)}, bf16[2,32,1024]{2,1,0:T(8,128)(2,1)S(1)}, u32[]{:S(2)}, u32[]{:S(2)}) %collective-permute-start.1) | collective-permute-done | bytes 131104 | tf_op jit(solution)/shard_map/while/body/eval_jaxpr/ppermute | solution.py:10
  433.5 10.4 %collective-permute-done.1 = bf16[2,32,1024]{2,1,0:T(8,128)(2,1)S(1)} collective-permute-done((bf16[2,32,1024]{2,1,0:T(8,128)(2,1)S(1)}, bf16[2,32,1024]{2,1,0:T(8,128)(2,1)S(1)}, u32[]{:S(2)}, u32[]{:S(2)}) %collective-permute-start.1) | collective-permute-done | bytes 131104 | tf_op jit(solution)/shard_map/while/body/eval_jaxpr/ppermute | solution.py:10
  448.9 10.4 %collective-permute-done.1 = bf16[2,32,1024]{2,1,0:T(8,128)(2,1)S(1)} collective-permute-done((bf16[2,32,1024]{2,1,0:T(8,128)(2,1)S(1)}, bf16[2,32,1024]{2,1,0:T(8,128)(2,1)S(1)}, u32[]{:S(2)}, u32[]{:S(2)}) %collective-permute-start.1) | collective-permute-done | bytes 131104 | tf_op jit(solution)/shard_map/while/body/eval_jaxpr/ppermute | solution.py:10
  461.6 7.4 %scatter_custom_fusion = f32[32,4096]{0,1:T(8,128)} fusion(s32[1024]{0:T(1024)S(1)} %bitcast.74, f32[1024,32]{1,0:T(8,128)S(1)} %copy.16, f32[]{:T(128)} %constant.58.clone.1), kind=kCustom, calls=%fused_computation.20 | custom fusion | flops 32768 | bytes 524292 | tf_op jit(solution)/shard_map/scatter-add | solution.py:72
  469.2 128.3 %reduce-scatter.2.cloned.1.call-done = f32[32,256]{0,1:T(8,128)} async-done(((f32[32,4096]{0,1:T(8,128)}), f32[32,256]{0,1:T(8,128)}) %reduce-scatter.2.cloned.1.call-update) | async-done | bytes 32784 | tf_op jit(solution)/shard_map/reduce_scatter | solution.py:73
  598.4 42.9 %all_gather.6 = bf16[32,4096]{0,1:T(8,128)(2,1)S(1)} all-gather(bf16[32,256]{0,1:T(8,128)(2,1)S(1)} %fusion.22), channel_id=1, replica_groups=mesh['panel'=16,'front'=16] {'front'}, dimensions={1}, use_global_device_ids=true | all-gather | bytes 278528 | tf_op jit(solution)/shard_map/all_gather | solution.py:77
  643.9 40.1 %all_gather.7 = bf16[32,4096]{1,0:T(8,128)(2,1)S(1)} all-gather(bf16[32,256]{1,0:T(8,128)(2,1)S(1)} %get-tuple-element.377), channel_id=1, replica_groups=mesh['panel'=16,'front'=16] {'front'}, dimensions={1}, use_global_device_ids=true | all-gather | bytes 278528 | tf_op jit(solution)/shard_map/all_gather | solution.py:81
  685.3 4.2 gather_fusion
  (195 shorter events, 190.5 us)
Async XLA Ops:
  7.2 590.3 %reduce-scatter.2.cloned.1.call-start = ((), (), s32[]{:S(2)}) async-start(), calls=%async_computation.1 | async-start | bytes 2228224 | tf_op jit(solution)/shard_map/reduce_scatter | solution.py:73
  10.6 6.3 collective-permute-start
  20.0 6.3 collective-permute-start
  29.5 6.3 collective-permute-start
  39.0 6.3 collective-permute-start
  48.5 6.3 collective-permute-start
  58.0 6.3 collective-permute-start
  77.0 11.0 %collective-permute-start = (bf16[2,32,1024]{2,1,0:T(8,128)(2,1)S(1)}, bf16[2,32,1024]{2,1,0:T(8,128)(2,1)S(1)}, u32[]{:S(2)}, u32[]{:S(2)}) collective-permute-start(bf16[2,32,1024]{2,1,0:T(8,128)(2,1)S(1)} %convolution_convert_fusion.2), channel_id=1, source_target_pairs={{0,16},{16,32},{32,48},{48,64},{64,80},{80,96},{96,112},{112,128},... | collective-permute-start | bytes 393224 | tf_op jit(solution)/shard_map/while/body/eval_jaxpr/ppermute | solution.py:10
  91.2 12.3 %collective-permute-start = (bf16[2,32,1024]{2,1,0:T(8,128)(2,1)S(1)}, bf16[2,32,1024]{2,1,0:T(8,128)(2,1)S(1)}, u32[]{:S(2)}, u32[]{:S(2)}) collective-permute-start(bf16[2,32,1024]{2,1,0:T(8,128)(2,1)S(1)} %convolution_convert_fusion.2), channel_id=1, source_target_pairs={{0,16},{16,32},{32,48},{48,64},{64,80},{80,96},{96,112},{112,128},... | collective-permute-start | bytes 393224 | tf_op jit(solution)/shard_map/while/body/eval_jaxpr/ppermute | solution.py:10
  106.7 12.3 %collective-permute-start = (bf16[2,32,1024]{2,1,0:T(8,128)(2,1)S(1)}, bf16[2,32,1024]{2,1,0:T(8,128)(2,1)S(1)}, u32[]{:S(2)}, u32[]{:S(2)}) collective-permute-start(bf16[2,32,1024]{2,1,0:T(8,128)(2,1)S(1)} %convolution_convert_fusion.2), channel_id=1, source_target_pairs={{0,16},{16,32},{32,48},{48,64},{64,80},{80,96},{96,112},{112,128},... | collective-permute-start | bytes 393224 | tf_op jit(solution)/shard_map/while/body/eval_jaxpr/ppermute | solution.py:10
  122.2 12.3 %collective-permute-start = (bf16[2,32,1024]{2,1,0:T(8,128)(2,1)S(1)}, bf16[2,32,1024]{2,1,0:T(8,128)(2,1)S(1)}, u32[]{:S(2)}, u32[]{:S(2)}) collective-permute-start(bf16[2,32,1024]{2,1,0:T(8,128)(2,1)S(1)} %convolution_convert_fusion.2), channel_id=1, source_target_pairs={{0,16},{16,32},{32,48},{48,64},{64,80},{80,96},{96,112},{112,128},... | collective-permute-start | bytes 393224 | tf_op jit(solution)/shard_map/while/body/eval_jaxpr/ppermute | solution.py:10
  137.7 12.3 %collective-permute-start = (bf16[2,32,1024]{2,1,0:T(8,128)(2,1)S(1)}, bf16[2,32,1024]{2,1,0:T(8,128)(2,1)S(1)}, u32[]{:S(2)}, u32[]{:S(2)}) collective-permute-start(bf16[2,32,1024]{2,1,0:T(8,128)(2,1)S(1)} %convolution_convert_fusion.2), channel_id=1, source_target_pairs={{0,16},{16,32},{32,48},{48,64},{64,80},{80,96},{96,112},{112,128},... | collective-permute-start | bytes 393224 | tf_op jit(solution)/shard_map/while/body/eval_jaxpr/ppermute | solution.py:10
  153.2 12.3 %collective-permute-start = (bf16[2,32,1024]{2,1,0:T(8,128)(2,1)S(1)}, bf16[2,32,1024]{2,1,0:T(8,128)(2,1)S(1)}, u32[]{:S(2)}, u32[]{:S(2)}) collective-permute-start(bf16[2,32,1024]{2,1,0:T(8,128)(2,1)S(1)} %convolution_convert_fusion.2), channel_id=1, source_target_pairs={{0,16},{16,32},{32,48},{48,64},{64,80},{80,96},{96,112},{112,128},... | collective-permute-start | bytes 393224 | tf_op jit(solution)/shard_map/while/body/eval_jaxpr/ppermute | solution.py:10
  168.7 12.3 %collective-permute-start = (bf16[2,32,1024]{2,1,0:T(8,128)(2,1)S(1)}, bf16[2,32,1024]{2,1,0:T(8,128)(2,1)S(1)}, u32[]{:S(2)}, u32[]{:S(2)}) collective-permute-start(bf16[2,32,1024]{2,1,0:T(8,128)(2,1)S(1)} %convolution_convert_fusion.2), channel_id=1, source_target_pairs={{0,16},{16,32},{32,48},{48,64},{64,80},{80,96},{96,112},{112,128},... | collective-permute-start | bytes 393224 | tf_op jit(solution)/shard_map/while/body/eval_jaxpr/ppermute | solution.py:10
  184.2 12.3 %collective-permute-start = (bf16[2,32,1024]{2,1,0:T(8,128)(2,1)S(1)}, bf16[2,32,1024]{2,1,0:T(8,128)(2,1)S(1)}, u32[]{:S(2)}, u32[]{:S(2)}) collective-permute-start(bf16[2,32,1024]{2,1,0:T(8,128)(2,1)S(1)} %convolution_convert_fusion.2), channel_id=1, source_target_pairs={{0,16},{16,32},{32,48},{48,64},{64,80},{80,96},{96,112},{112,128},... | collective-permute-start | bytes 393224 | tf_op jit(solution)/shard_map/while/body/eval_jaxpr/ppermute | solution.py:10
  199.7 12.3 %collective-permute-start = (bf16[2,32,1024]{2,1,0:T(8,128)(2,1)S(1)}, bf16[2,32,1024]{2,1,0:T(8,128)(2,1)S(1)}, u32[]{:S(2)}, u32[]{:S(2)}) collective-permute-start(bf16[2,32,1024]{2,1,0:T(8,128)(2,1)S(1)} %convolution_convert_fusion.2), channel_id=1, source_target_pairs={{0,16},{16,32},{32,48},{48,64},{64,80},{80,96},{96,112},{112,128},... | collective-permute-start | bytes 393224 | tf_op jit(solution)/shard_map/while/body/eval_jaxpr/ppermute | solution.py:10
  215.1 12.2 %collective-permute-start.1 = (bf16[2,32,1024]{2,1,0:T(8,128)(2,1)S(1)}, bf16[2,32,1024]{2,1,0:T(8,128)(2,1)S(1)}, u32[]{:S(2)}, u32[]{:S(2)}) collective-permute-start(bf16[2,32,1024]{2,1,0:T(8,128)(2,1)S(1)} %get-tuple-element.467), channel_id=1, source_target_pairs={{16,0},{32,16},{48,32},{64,48},{80,64},{96,80},{112,96},{128,112},... | collective-permute-start | bytes 393224 | tf_op jit(solution)/shard_map/while/body/eval_jaxpr/ppermute | solution.py:10
  230.3 13.0 %collective-permute-start.1 = (bf16[2,32,1024]{2,1,0:T(8,128)(2,1)S(1)}, bf16[2,32,1024]{2,1,0:T(8,128)(2,1)S(1)}, u32[]{:S(2)}, u32[]{:S(2)}) collective-permute-start(bf16[2,32,1024]{2,1,0:T(8,128)(2,1)S(1)} %get-tuple-element.467), channel_id=1, source_target_pairs={{16,0},{32,16},{48,32},{64,48},{80,64},{96,80},{112,96},{128,112},... | collective-permute-start | bytes 393224 | tf_op jit(solution)/shard_map/while/body/eval_jaxpr/ppermute | solution.py:10
  246.4 12.2 %collective-permute-start.1 = (bf16[2,32,1024]{2,1,0:T(8,128)(2,1)S(1)}, bf16[2,32,1024]{2,1,0:T(8,128)(2,1)S(1)}, u32[]{:S(2)}, u32[]{:S(2)}) collective-permute-start(bf16[2,32,1024]{2,1,0:T(8,128)(2,1)S(1)} %get-tuple-element.467), channel_id=1, source_target_pairs={{16,0},{32,16},{48,32},{64,48},{80,64},{96,80},{112,96},{128,112},... | collective-permute-start | bytes 393224 | tf_op jit(solution)/shard_map/while/body/eval_jaxpr/ppermute | solution.py:10
  261.6 13.0 %collective-permute-start.1 = (bf16[2,32,1024]{2,1,0:T(8,128)(2,1)S(1)}, bf16[2,32,1024]{2,1,0:T(8,128)(2,1)S(1)}, u32[]{:S(2)}, u32[]{:S(2)}) collective-permute-start(bf16[2,32,1024]{2,1,0:T(8,128)(2,1)S(1)} %get-tuple-element.467), channel_id=1, source_target_pairs={{16,0},{32,16},{48,32},{64,48},{80,64},{96,80},{112,96},{128,112},... | collective-permute-start | bytes 393224 | tf_op jit(solution)/shard_map/while/body/eval_jaxpr/ppermute | solution.py:10
  277.6 12.2 %collective-permute-start.1 = (bf16[2,32,1024]{2,1,0:T(8,128)(2,1)S(1)}, bf16[2,32,1024]{2,1,0:T(8,128)(2,1)S(1)}, u32[]{:S(2)}, u32[]{:S(2)}) collective-permute-start(bf16[2,32,1024]{2,1,0:T(8,128)(2,1)S(1)} %get-tuple-element.467), channel_id=1, source_target_pairs={{16,0},{32,16},{48,32},{64,48},{80,64},{96,80},{112,96},{128,112},... | collective-permute-start | bytes 393224 | tf_op jit(solution)/shard_map/while/body/eval_jaxpr/ppermute | solution.py:10
  292.8 13.0 %collective-permute-start.1 = (bf16[2,32,1024]{2,1,0:T(8,128)(2,1)S(1)}, bf16[2,32,1024]{2,1,0:T(8,128)(2,1)S(1)}, u32[]{:S(2)}, u32[]{:S(2)}) collective-permute-start(bf16[2,32,1024]{2,1,0:T(8,128)(2,1)S(1)} %get-tuple-element.467), channel_id=1, source_target_pairs={{16,0},{32,16},{48,32},{64,48},{80,64},{96,80},{112,96},{128,112},... | collective-permute-start | bytes 393224 | tf_op jit(solution)/shard_map/while/body/eval_jaxpr/ppermute | solution.py:10
  308.9 12.3 %collective-permute-start.1 = (bf16[2,32,1024]{2,1,0:T(8,128)(2,1)S(1)}, bf16[2,32,1024]{2,1,0:T(8,128)(2,1)S(1)}, u32[]{:S(2)}, u32[]{:S(2)}) collective-permute-start(bf16[2,32,1024]{2,1,0:T(8,128)(2,1)S(1)} %get-tuple-element.467), channel_id=1, source_target_pairs={{16,0},{32,16},{48,32},{64,48},{80,64},{96,80},{112,96},{128,112},... | collective-permute-start | bytes 393224 | tf_op jit(solution)/shard_map/while/body/eval_jaxpr/ppermute | solution.py:10
  324.2 12.3 %collective-permute-start.1 = (bf16[2,32,1024]{2,1,0:T(8,128)(2,1)S(1)}, bf16[2,32,1024]{2,1,0:T(8,128)(2,1)S(1)}, u32[]{:S(2)}, u32[]{:S(2)}) collective-permute-start(bf16[2,32,1024]{2,1,0:T(8,128)(2,1)S(1)} %get-tuple-element.467), channel_id=1, source_target_pairs={{16,0},{32,16},{48,32},{64,48},{80,64},{96,80},{112,96},{128,112},... | collective-permute-start | bytes 393224 | tf_op jit(solution)/shard_map/while/body/eval_jaxpr/ppermute | solution.py:10
  339.6 12.3 %collective-permute-start.1 = (bf16[2,32,1024]{2,1,0:T(8,128)(2,1)S(1)}, bf16[2,32,1024]{2,1,0:T(8,128)(2,1)S(1)}, u32[]{:S(2)}, u32[]{:S(2)}) collective-permute-start(bf16[2,32,1024]{2,1,0:T(8,128)(2,1)S(1)} %get-tuple-element.467), channel_id=1, source_target_pairs={{16,0},{32,16},{48,32},{64,48},{80,64},{96,80},{112,96},{128,112},... | collective-permute-start | bytes 393224 | tf_op jit(solution)/shard_map/while/body/eval_jaxpr/ppermute | solution.py:10
  354.9 12.3 %collective-permute-start.1 = (bf16[2,32,1024]{2,1,0:T(8,128)(2,1)S(1)}, bf16[2,32,1024]{2,1,0:T(8,128)(2,1)S(1)}, u32[]{:S(2)}, u32[]{:S(2)}) collective-permute-start(bf16[2,32,1024]{2,1,0:T(8,128)(2,1)S(1)} %get-tuple-element.467), channel_id=1, source_target_pairs={{16,0},{32,16},{48,32},{64,48},{80,64},{96,80},{112,96},{128,112},... | collective-permute-start | bytes 393224 | tf_op jit(solution)/shard_map/while/body/eval_jaxpr/ppermute | solution.py:10
  370.2 12.3 %collective-permute-start.1 = (bf16[2,32,1024]{2,1,0:T(8,128)(2,1)S(1)}, bf16[2,32,1024]{2,1,0:T(8,128)(2,1)S(1)}, u32[]{:S(2)}, u32[]{:S(2)}) collective-permute-start(bf16[2,32,1024]{2,1,0:T(8,128)(2,1)S(1)} %get-tuple-element.467), channel_id=1, source_target_pairs={{16,0},{32,16},{48,32},{64,48},{80,64},{96,80},{112,96},{128,112},... | collective-permute-start | bytes 393224 | tf_op jit(solution)/shard_map/while/body/eval_jaxpr/ppermute | solution.py:10
  385.6 12.3 %collective-permute-start.1 = (bf16[2,32,1024]{2,1,0:T(8,128)(2,1)S(1)}, bf16[2,32,1024]{2,1,0:T(8,128)(2,1)S(1)}, u32[]{:S(2)}, u32[]{:S(2)}) collective-permute-start(bf16[2,32,1024]{2,1,0:T(8,128)(2,1)S(1)} %get-tuple-element.467), channel_id=1, source_target_pairs={{16,0},{32,16},{48,32},{64,48},{80,64},{96,80},{112,96},{128,112},... | collective-permute-start | bytes 393224 | tf_op jit(solution)/shard_map/while/body/eval_jaxpr/ppermute | solution.py:10
  400.9 12.3 %collective-permute-start.1 = (bf16[2,32,1024]{2,1,0:T(8,128)(2,1)S(1)}, bf16[2,32,1024]{2,1,0:T(8,128)(2,1)S(1)}, u32[]{:S(2)}, u32[]{:S(2)}) collective-permute-start(bf16[2,32,1024]{2,1,0:T(8,128)(2,1)S(1)} %get-tuple-element.467), channel_id=1, source_target_pairs={{16,0},{32,16},{48,32},{64,48},{80,64},{96,80},{112,96},{128,112},... | collective-permute-start | bytes 393224 | tf_op jit(solution)/shard_map/while/body/eval_jaxpr/ppermute | solution.py:10
  416.3 12.3 %collective-permute-start.1 = (bf16[2,32,1024]{2,1,0:T(8,128)(2,1)S(1)}, bf16[2,32,1024]{2,1,0:T(8,128)(2,1)S(1)}, u32[]{:S(2)}, u32[]{:S(2)}) collective-permute-start(bf16[2,32,1024]{2,1,0:T(8,128)(2,1)S(1)} %get-tuple-element.467), channel_id=1, source_target_pairs={{16,0},{32,16},{48,32},{64,48},{80,64},{96,80},{112,96},{128,112},... | collective-permute-start | bytes 393224 | tf_op jit(solution)/shard_map/while/body/eval_jaxpr/ppermute | solution.py:10
  431.6 12.3 %collective-permute-start.1 = (bf16[2,32,1024]{2,1,0:T(8,128)(2,1)S(1)}, bf16[2,32,1024]{2,1,0:T(8,128)(2,1)S(1)}, u32[]{:S(2)}, u32[]{:S(2)}) collective-permute-start(bf16[2,32,1024]{2,1,0:T(8,128)(2,1)S(1)} %get-tuple-element.467), channel_id=1, source_target_pairs={{16,0},{32,16},{48,32},{64,48},{80,64},{96,80},{112,96},{128,112},... | collective-permute-start | bytes 393224 | tf_op jit(solution)/shard_map/while/body/eval_jaxpr/ppermute | solution.py:10
  446.9 12.3 %collective-permute-start.1 = (bf16[2,32,1024]{2,1,0:T(8,128)(2,1)S(1)}, bf16[2,32,1024]{2,1,0:T(8,128)(2,1)S(1)}, u32[]{:S(2)}, u32[]{:S(2)}) collective-permute-start(bf16[2,32,1024]{2,1,0:T(8,128)(2,1)S(1)} %get-tuple-element.467), channel_id=1, source_target_pairs={{16,0},{32,16},{48,32},{64,48},{80,64},{96,80},{112,96},{128,112},... | collective-permute-start | bytes 393224 | tf_op jit(solution)/shard_map/while/body/eval_jaxpr/ppermute | solution.py:10
  (37 other events, 1237.9 us)
Sparse Core Ops, SparseCore 0:
  469.2 128.2 reduce-scatter.1
where the time goes:
time: 699 us; the launch traced here: 698 us
  waiting for transfers between devices  331 us (47%)
  starting transfers between devices  147 us (21%)
  matrix products  105 us (15%)
  blocking collectives  82.9 us (12%)
  between operations  14.2 us (2%)
  other arithmetic  10.2 us (1%)
    ppermute x32, waiting for transfers between devices, shifted(): return lax.ppermute(block, axis, route)  202 us
    ppermute x32, starting transfers between devices, shifted(): return lax.ppermute(block, axis, route)  147 us
    reduce_scatter x1, waiting for transfers between devices, local(): lax.psum_scatter(placed, 'front', scatter_dimension=1, tiled=True)  128 us
    dot_general x32, matrix products, leaf_apply(): jnp.einsum('fbl,flm->fbm', loaded.astype(jnp.bfloat16), inverse, preferre...  98.8 us
    all_gather x1, blocking collectives, local(): lax.all_gather(reduced, 'front', axis=1, tiled=True)  42.9 us
    all_gather x1, blocking collectives, local(): lax.all_gather(sep_solved.astype(jnp.bfloat16), 'front', axis=1, tiled=True)  40.1 us
  transfers between devices with their start and end apart: 33, of which 33 were waited for; matrix products, arithmetic and copies ran while one was open for 0% of the time, Pallas kernels for 0%

commit v1 on v0

v1 whole, which is shorter than its diff:
```python
import jax
import jax.numpy as jnp
from jax import lax
from jax.experimental import pallas as pl
from jax.experimental.pallas import tpu as pltpu
from jax.sharding import PartitionSpec as P

MESH = pl.DeviceIdType.MESH
F32 = jnp.float32
BF16 = jnp.bfloat16
LEAF = 1024
UPD = 512
SHARE = 256
RHS = 32
ROWS = 32
PEERS = 16
LAST = 7
DIRECT = 3
HALF = 16
WAVES = 4
CHUNK = 256
CHUNKS = LEAF // CHUNK

S_CP, S_SRC, S_A, S_PM, S_SS, S_LIFT, S_SEP, S_P, S_Q, S_UA, S_OUT = 0, 1, 2, 4, 5, 6, 7, 8, 10, 12, 13


def dot(a, b):
    return jnp.dot(a, b, preferred_element_type=F32)


def dot_t(a, b):
    return lax.dot_general(a, b, (((1,), (1,)), ((), ())), preferred_element_type=F32)


def kernel(
    src, ssep, inv, lift, lower, sepinv, pm, cd, cu,
    leaf_out, sep_out,
    A, PP, QQ, LL, LW, SS, SL, CP, CT, PM, SRC_S,
    T, U, TS, US, E, DB, G, UA, UB,
    Z, PMS, PMR, UPS, UPR, ONE, RED, PKS, PKR, SEPA,
    lsem, ps, pr, dsnd, drcv, usnd, urcv, asnd, arcv,
):
    p = lax.axis_index("panel")
    me = lax.axis_index("front")
    core = lax.rem(p, 2)
    c = p // 2
    pair = (p + 1 - 2 * core, me)
    is0 = core == 0
    is1 = core == 1
    first = c == 0
    last = c == LAST

    def remote(s, d, ss, rs, dev):
        return pltpu.make_async_remote_copy(
            src_ref=s, dst_ref=d, send_sem=ss, recv_sem=rs, device_id=dev, device_id_type=MESH
        )

    def to_pair(s, d, i):
        return remote(s, d, ps.at[i], pr.at[i], pair)

    own = [pltpu.make_async_copy(inv.at[f], A.at[core, f], lsem.at[f]) for f in range(2)]
    own_lift = pltpu.make_async_copy(lift, LL.at[1], lsem.at[2])
    own_lower = pltpu.make_async_copy(lower, LW, lsem.at[3])
    own_sep = pltpu.make_async_copy(sepinv, SS.at[1], lsem.at[4])
    for copy in own:
        copy.start()

    barrier = pltpu.get_barrier_semaphore()

    def greet(k, _):
        pl.semaphore_signal(
            barrier, inc=1, device_id=(2 * c + 1, lax.rem(me + k, PEERS)), device_id_type=MESH
        )
        return 0

    @pl.when(is0)
    def _():
        greet(0, 0)

    @pl.when(is1)
    def _():
        pl.semaphore_signal(barrier, inc=1, device_id=pair, device_id_type=MESH)

        @pl.when(c > 0)
        def _():
            pl.semaphore_signal(barrier, inc=1, device_id=(p - 2, me), device_id_type=MESH)

        @pl.when(c < LAST)
        def _():
            pl.semaphore_signal(barrier, inc=1, device_id=(p + 2, me), device_id_type=MESH)

    lax.fori_loop(1, PEERS, greet, 0)
    CP[core, 0:2, :] = cd[...]
    CP[core, 2:4, :] = cu[...]
    PM[core, 0:2, :] = pm[...].astype(F32)
    ends = jnp.where(first, 0, 1) + jnp.where(last, 0, 1)
    pl.semaphore_wait(barrier, jnp.where(is1, 2 * PEERS - 1 + ends, 1))

    send_a = [to_pair(inv.at[f], A.at[core, f], S_A + f) for f in range(2)]
    got_a = [to_pair(inv.at[f], A.at[1 - core, f], S_A + f) for f in range(2)]
    send_cp = to_pair(CP.at[core], CP.at[core], S_CP)
    got_cp = to_pair(CP.at[core], CP.at[1 - core], S_CP)
    send_src = to_pair(src, SL, S_SRC)
    send_pm = to_pair(PM.at[0], PM.at[0], S_PM)
    send_ss = to_pair(ssep, SRC_S, S_SS)
    send_lift = to_pair(lift, LL.at[0], S_LIFT)
    send_sep = to_pair(sepinv, SS.at[0], S_SEP)
    ship_p = [to_pair(PP.at[f], PP.at[f], S_P + f) for f in range(2)]
    ship_q = [to_pair(QQ.at[f], QQ.at[f], S_Q + f) for f in range(2)]
    ship_ua = to_pair(UA, UA, S_UA)
    ship_out = to_pair(SEPA, SEPA, S_OUT)

    send_cp.start()

    def finish(x, sweep):
        pt = PKR[...].astype(F32).reshape(UPD, 128).T.astype(BF16)
        for f in range(2):
            r = (2 * x + f) * RHS
            leaf_out[f] = sweep[f] - dot(pt[r : r + RHS, :], LW[f])

    @pl.when(is0)
    def _core0():
        send_src.start()
        send_a[0].start()
        send_a[1].start()
        send_pm.start()
        send_ss.start()
        own_lower.start()
        got_cp.wait_recv()
        for x in range(2):
            CT[x] = CP[x].T
        for f in range(2):
            own[f].wait()
            got_a[f].wait_recv()

            @pl.loop(0, 4)
            def _(b):
                rows = pl.ds(pl.multiple_of(b * 256, 256), 256)
                left = (A[0, f, rows, :].astype(F32) * CP[1, f : f + 1, :]).astype(BF16)
                PP[f, rows, :] = (dot(left, A[1, f]) * CT[0, rows, f : f + 1]).astype(BF16)
                to_pair(PP.at[f, rows], PP.at[f, rows], S_P + f).start()

        send_lift.start()
        send_sep.start()
        for f in range(2):

            @pl.loop(0, 4)
            def _(b):
                rows = pl.ds(pl.multiple_of(b * 256, 256), 256)
                base = jnp.where(last, PP[f, rows, :].astype(F32), A[1, f, rows, :].astype(F32))
                left = (base * CP[0, f + 2 : f + 3, :]).astype(BF16)
                scale = jnp.where(last, 1.0, CT[1, rows, f + 2 : f + 3])
                extra = jnp.where(last, CT[0, rows, f : f + 1], 0.0)
                full = dot(left, A[0, f]) * scale + extra * A[0, f, rows, :].astype(F32)
                QQ[f, rows, :] = full.astype(BF16)
                to_pair(QQ.at[f, rows], QQ.at[f, rows], S_Q + f).start()

        for copy in (send_cp, send_src, *send_a, send_pm, send_ss, send_lift, send_sep, *ship_p, *ship_q):
            copy.wait_send()
        own_lower.wait()
        ship_ua.wait_recv()
        ship_out.wait_recv()
        sep_out[...] = SEPA[...]
        remote(PKR, PKR, asnd.at[3], arcv.at[3], pair).wait_recv()
        finish(0, UA)

    def wave_of(w):
        return w // 2, pl.ds(pl.multiple_of(lax.rem(w, 2) * HALF, HALF), HALF)

    @pl.when(is1)
    def _core1():
        send_a[0].start()
        send_a[1].start()
        own_lift.start()
        own_sep.start()
        own_lower.start()

        below = (p + 2, me)
        above = (p - 2, me)

        def down_wave(w, cols=slice(None)):
            f, rows = wave_of(w)
            return remote(TS.at[f, rows, cols], T.at[f, rows, cols], dsnd.at[w], drcv.at[w], below)

        def up_wave(w, cols=slice(None)):
            f, rows = wave_of(w)
            return remote(US.at[f, rows, cols], U.at[f, rows, cols], usnd.at[w], urcv.at[w], above)

        def coupled(x, f, k):
            return CP[x, pl.ds(f + k, 1), :]

        got_cp.wait_recv()
        send_pm.wait_recv()
        Z[...] = jnp.zeros_like(Z)
        Z[0:2, :] = PM[0, 0:2, :]
        Z[2:4, :] = PM[1, 0:2, :]
        PMS[...] = Z[...].T

        def exchange(k, out, into, lane, target_core):
            o = lax.rem(me + k, PEERS)
            rows = pl.ds(pl.multiple_of(o * ROWS, ROWS), ROWS)
            return remote(
                out.at[rows], into.at[me], asnd.at[lane], arcv.at[lane], (2 * c + target_core, o)
            )

        def all_to_all(out, into, lane):
            def one(k, _):
                exchange(k, out, into, lane, 1).start()
                return 0

            lax.fori_loop(1, PEERS, one, 0)
            into[me] = out[pl.ds(pl.multiple_of(me * ROWS, ROWS), ROWS), :]

        def arrived(into, lane):
            part = into.at[pl.ds(0, PEERS - 1)]
            return remote(part, part, asnd.at[lane], arcv.at[lane], pair)

        all_to_all(PMS, PMR, 0)

        def build_maps():
            arrived(PMR, 0).wait()
            table = PMR[...].reshape(UPD, 128)
            column = (lax.broadcasted_iota(jnp.int32, (UPD, SHARE), 1) + me * SHARE).astype(F32)
            for q in range(4):
                ONE[q] = jnp.where(table[:, q : q + 1] == column, 1.0, 0.0).astype(BF16)

        send_src.wait_recv()
        for f in range(2):
            got_a[f].wait_recv()
            own[f].wait()

        @pl.when(first)
        def _():
            T[...] = jnp.zeros_like(T)

        @pl.when(c <= DIRECT)
        def _():
            def step(w, _):
                f, rows = wave_of(w)

                @pl.when(c > 0)
                def _():
                    down_wave(w).wait_recv()

                loaded = SL[f, rows, :] + coupled(0, f, 0) * T[f, rows, :].astype(F32)
                middle = dot(loaded.astype(BF16), A[0, f])
                loaded = src[f, rows, :] + coupled(1, f, 0) * middle.astype(BF16).astype(F32)
                loaded = loaded.astype(BF16)
                for j in range(CHUNKS):
                    cols = slice(j * CHUNK, (j + 1) * CHUNK)
                    out = dot(loaded, A[1, f, :, cols])
                    DB[f, rows, cols] = out
                    TS[f, rows, cols] = out.astype(BF16)
                    down_wave(w, cols).start()
                return 0

            lax.fori_loop(0, WAVES, step, 0)
            build_maps()

        @pl.when(c > DIRECT)
        def _():
            def alone(f, _):
                middle = dot(SL[f].astype(BF16), A[0, f])
                loaded = src[f] + coupled(1, f, 0) * middle.astype(BF16).astype(F32)
                out = dot(loaded.astype(BF16), A[1, f])
                DB[f] = out
                E[f] = out

                @pl.when(last)
                def _():
                    loaded = SL[f] + coupled(0, f, 2) * out.astype(BF16).astype(F32)
                    E[f] = dot(loaded.astype(BF16), A[0, f])

                return 0

            lax.fori_loop(0, 2, alone, 0)
            build_maps()

            def sweep(weight, keep, half, copy_of):
                def step(w, _):
                    f, rows = wave_of(w)
                    down_wave(w).wait_recv()
                    t = T[f, rows, :]
                    for j in range(CHUNKS):
                        cols = slice(j * CHUNK, (j + 1) * CHUNK)
                        out = dot(t, weight[f, :, cols]) + E[f, rows, cols]
                        keep[f, rows, cols] = out
                        half[f, rows, cols] = out.astype(BF16)
                        copy_of(w, cols).start()
                    return 0

                lax.fori_loop(0, WAVES, step, 0)

            for f in range(2):
                ship_p[f].wait_recv()

            @pl.when(c < LAST)
            def _():
                sweep(PP, DB, TS, down_wave)

            @pl.when(last)
            def _():
                for f in range(2):
                    ship_q[f].wait_recv()
                sweep(QQ, UA, US, up_wave)

                def rest(f, _):
                    UB[f] = DB[f] + dot(T[f], PP[f])
                    return 0

                lax.fori_loop(0, 2, rest, 0)

        @pl.when(c <= DIRECT)
        def _():
            for f in range(2):
                ship_p[f].wait_recv()

        @pl.when(c < LAST)
        def _():
            def before(f, _):
                loaded = (
                    SL[f]
                    + coupled(0, f, 0) * T[f].astype(F32)
                    + coupled(0, f, 2) * DB[f].astype(BF16).astype(F32)
                )
                G[f] = dot(loaded.astype(BF16), A[0, f])
                return 0

            lax.fori_loop(0, 2, before, 0)
            for f in range(2):
                ship_q[f].wait_recv()

            def step(w, _):
                f, rows = wave_of(w)
                up_wave(w).wait_recv()
                t = U[f, rows, :]
                for j in range(CHUNKS):
                    cols = slice(j * CHUNK, (j + 1) * CHUNK)
                    out = dot(t, QQ[f, :, cols]) + G[f, rows, cols]
                    UA[f, rows, cols] = out
                    US[f, rows, cols] = out.astype(BF16)

                    @pl.when(c > 0)
                    def _():
                        up_wave(w, cols).start()

                return 0

            lax.fori_loop(0, WAVES, step, 0)

            def rest(f, _):
                loaded = coupled(1, f, 2) * U[f].astype(F32)
                UB[f] = DB[f] + dot(loaded.astype(BF16), A[1, f])
                return 0

            lax.fori_loop(0, 2, rest, 0)

        ship_ua.start()
        send_lift.wait_recv()
        own_lift.wait()
        for x, swept in enumerate((UA, UB)):
            for f in range(2):
                r = (2 * x + f) * RHS
                Z[r : r + RHS, :] = dot(swept[f].astype(BF16), LL[x, f])
        UPS[...] = Z[...].T.astype(BF16)
        all_to_all(UPS, UPR, 1)
        send_ss.wait_recv()
        arrived(UPR, 1).wait()
        updates = UPR[...].astype(F32).reshape(UPD, 128).T.astype(BF16)
        for x, source in enumerate((SRC_S, ssep)):
            r = 2 * x * RHS
            gathered = dot(updates[r : r + RHS, :], ONE[2 * x])
            gathered += dot(updates[r + RHS : r + 2 * RHS, :], ONE[2 * x + 1])
            RED[me, x * RHS : (x + 1) * RHS, :] = (source[...] - gathered).astype(BF16)

        def spread(k, _):
            o = lax.rem(me + k, PEERS)
            remote(RED.at[me], RED.at[me], asnd.at[2], arcv.at[2], (p, o)).start()
            return 0

        lax.fori_loop(1, PEERS, spread, 0)
        send_sep.wait_recv()
        own_sep.wait()
        arrived(RED, 2).wait()
        for x in range(2):
            total = jnp.zeros((RHS, SHARE), F32)
            for s in range(PEERS):
                total += dot(
                    RED[s, x * RHS : (x + 1) * RHS, :], SS[x, s * SHARE : (s + 1) * SHARE, :]
                )
            if x == 0:
                SEPA[...] = total
            else:
                sep_out[...] = total
            half = total.astype(BF16)
            for f in range(2):
                r = (2 * x + f) * RHS
                Z[r : r + RHS, :] = dot_t(half, ONE[2 * x + f])
        PKS[...] = Z[...].T.astype(BF16)
        ship_out.start()

        def pick(k, _):
            exchange(k, PKS, PKR, 3, 0).start()
            return 0

        lax.fori_loop(0, PEERS, pick, 0)
        all_to_all(PKS, PKR, 4)
        own_lower.wait()
        arrived(PKR, 4).wait()
        finish(1, UB)

        for copy in (send_cp, *send_a, ship_ua, ship_out):
            copy.wait_send()
        remote(PKR, PKR, asnd.at[3], arcv.at[3], pair).wait_send()

        def sent_down(w, _):
            down_wave(w).wait_send()
            return 0

        def sent_up(w, _):
            up_wave(w).wait_send()
            return 0

        @pl.when(c < LAST)
        def _():
            lax.fori_loop(0, WAVES, sent_down, 0)

        @pl.when(c > 0)
        def _():
            lax.fori_loop(0, WAVES, sent_up, 0)


def local(source_leaf, source_sep, leaf_inverse, lift, lower, sep_inverse, parent_map, couple_down, couple_up):
    vmem = pl.BlockSpec(memory_space=pltpu.VMEM)
    hbm = pl.BlockSpec(memory_space=pl.ANY)
    trace = (2, RHS, LEAF)
    leaf, sep = pl.pallas_call(
        kernel,
        out_shape=(
            jax.ShapeDtypeStruct(trace, F32),
            jax.ShapeDtypeStruct((RHS, SHARE), F32),
        ),
        in_specs=[vmem, vmem, hbm, hbm, hbm, hbm, vmem, vmem, vmem],
        out_specs=(vmem, vmem),
        scratch_shapes=[
            pltpu.VMEM((2, 2, LEAF, LEAF), BF16),
            pltpu.VMEM((2, LEAF, LEAF), BF16),
            pltpu.VMEM((2, LEAF, LEAF), BF16),
            pltpu.VMEM((2, 2, LEAF, UPD), BF16),
            pltpu.VMEM((2, UPD, LEAF), BF16),
            pltpu.VMEM((2, PEERS * SHARE, SHARE), BF16),
            pltpu.VMEM(trace, F32),
            pltpu.VMEM((2, 8, LEAF), F32),
            pltpu.VMEM((2, LEAF, 8), F32),
            pltpu.VMEM((2, 8, UPD), F32),
            pltpu.VMEM((RHS, SHARE), F32),
            *[pltpu.VMEM(trace, BF16) for _ in range(4)],
            *[pltpu.VMEM(trace, F32) for _ in range(5)],
            pltpu.VMEM((128, UPD), F32),
            pltpu.VMEM((UPD, 128), F32),
            pltpu.VMEM((PEERS, ROWS, 128), F32),
            pltpu.VMEM((UPD, 128), BF16),
            pltpu.VMEM((PEERS, ROWS, 128), BF16),
            pltpu.VMEM((4, UPD, SHARE), BF16),
            pltpu.VMEM((PEERS, 2 * RHS, SHARE), BF16),
            pltpu.VMEM((UPD, 128), BF16),
            pltpu.VMEM((PEERS, ROWS, 128), BF16),
            pltpu.VMEM((RHS, SHARE), F32),
            pltpu.SemaphoreType.DMA((5,)),
            pltpu.SemaphoreType.DMA((14,)),
            pltpu.SemaphoreType.DMA((14,)),
            pltpu.SemaphoreType.DMA((WAVES,)),
            pltpu.SemaphoreType.DMA((WAVES,)),
            pltpu.SemaphoreType.DMA((WAVES,)),
            pltpu.SemaphoreType.DMA((WAVES,)),
            pltpu.SemaphoreType.DMA((5,)),
            pltpu.SemaphoreType.DMA((5,)),
        ],
        compiler_params=pltpu.CompilerParams(
            collective_id=0, has_side_effects=True, vmem_limit_bytes=56 * 1024 * 1024
        ),
        name="sweep",
    )(
        source_leaf[0], source_sep[0], leaf_inverse[0], lift[0], lower[0],
        sep_inverse[0], parent_map[0], couple_down[0], couple_up[0],
    )
    return leaf[None], sep[None]


def solution(mesh):
    return jax.shard_map(
        local,
        mesh=mesh,
        in_specs=(
            P("panel", "front", None, None),
            P("panel", None, "front"),
            P("panel", "front", None, None),
            P("panel", "front", None, None),
            P("panel", "front", None, None),
            P("panel", None, "front"),
            P("panel", "front", None),
            P("panel", "front", None),
            P("panel", "front", None),
        ),
        out_specs=(P("panel", "front", None, None), P("panel", None, "front")),
        check_vma=False,
    )
```

time: 699 us -> 92.7 us (0.13)
  the two profiles are of different devices: /device:TPU:8 before, /device:TPU:1 now
where the time goes in v1:
time: 92.7 us; the launch traced here: 92.5 us
  Pallas kernels  88.8 us (96%)
  local copies, waits for them, and re-layouts  3.05 us (3%)
    pallas_call x1, Pallas kernels, local(): pl.pallas_call(kernel, out_shape=(jax.ShapeDtypeStruct(trace, F32), jax.S...  88.8 us
    unnamed x2, local copies, waits for them, and re-layouts  3.05 us

profile of v1, /device:TPU:1, one launch (start us, length us, event | category | flops | bytes accessed | tf_op | source)
XLA Modules:
  0.0 92.5 jit_solution(16858964793270356597)
XLA Ops:
  0.6 88.8 %sweep.1 = (f32[2,32,1024]{2,1,0:T(8,128)}, f32[32,256]{1,0:T(8,128)}) custom-call(f32[2,32,1024]{2,1,0:T(8,128)} %bitcast.15, f32[32,256]{1,0:T(8,128)} %bitcast.17, bf16[2,1024,1024]{2,1,0:T(8,128)(2,1)} %bitcast.11, bf16[2,1024,512]{2,1,0:T(8,128)(2,1)} %bitcast.12, bf16[2,512,1024]{2,1,0:T(8,128)(2,1)} %bitcast.13, bf16[4096,256]{1,0:T(8,128)(2,1)} %bitcast.14, ...), custom_call_target="tpu_custom_call" | custom-call | tf_op jit(solution)/shard_map/sweep/pallas_call | solution.py:437
  89.5 1.7 %copy.13 = f32[1,2,32,1024]{3,2,1,0:T(8,128)} copy(f32[1,2,32,1024]{3,2,1,0:T(8,128)} %bitcast.16) | data formatting | bytes 524288
  91.1 1.4 %copy.14 = f32[1,32,256]{2,1,0:T(8,128)} copy(f32[1,32,256]{2,1,0:T(8,128)} %bitcast.18) | data formatting | bytes 65536

commit v2 on v1

v2 whole, which is shorter than its diff:
```python
import functools

import jax
import jax.numpy as jnp
from jax import lax
from jax.experimental import pallas as pl
from jax.experimental.pallas import tpu as pltpu
from jax.sharding import PartitionSpec as P

MESH = pl.DeviceIdType.MESH
F32 = jnp.float32
BF16 = jnp.bfloat16
LEAF = 1024
UPD = 512
SHARE = 256
RHS = 32
ROWS = 16
GROUP = 4
PEERS = 16
LAST = 7
DIRECT = 3
HALF = 16
WAVES = 4
CHUNK = 512
CHUNKS = LEAF // CHUNK

S_CP, S_SRC, S_A, S_LIFT, S_P, S_Q, S_UA, S_DA = 0, 1, 2, 4, 5, 7, 9, 10


def dot(a, b):
    return jnp.dot(a, b, preferred_element_type=F32)


def dot_t(a, b):
    return lax.dot_general(a, b, (((1,), (1,)), ((), ())), preferred_element_type=F32)


def kernel(
    src, ssep, inv, lift, lower, sepinv, pm, cd, cu,
    leaf_out, sep_out,
    A, PP, QQ, LL, LW, SS, SL, CP, CT,
    T, U, TS, US, DA, E, DB, G, UA, UB,
    Z, ZP, PMS, PMR, UPS, UPR, ONE, RED, PKS, PKR,
    lsem, ps, pr, dsnd, drcv, usnd, urcv, osnd, orcv, rsnd, rrcv,
):
    p = lax.axis_index("panel")
    me = lax.axis_index("front")
    core = lax.rem(p, 2)
    c = p // 2
    pair = (p + 1 - 2 * core, me)
    is0 = core == 0
    is1 = core == 1
    first = c == 0
    last = c == LAST
    def remote(s, d, ss, rs, dev):
        return pltpu.make_async_remote_copy(
            src_ref=s, dst_ref=d, send_sem=ss, recv_sem=rs, device_id=dev, device_id_type=MESH
        )

    def to_pair(s, d, i):
        return remote(s, d, ps.at[i], pr.at[i], pair)

    own = [pltpu.make_async_copy(inv.at[f], A.at[core, f], lsem.at[f]) for f in range(2)]
    own_lift = pltpu.make_async_copy(lift, LL.at[1], lsem.at[2])
    own_lower = [
        pltpu.make_async_copy(lower.at[f, :, h], LW.at[f, h], lsem.at[4 + 2 * f + h])
        for f in range(2)
        for h in range(2)
    ]
    own_sep = pltpu.make_async_copy(sepinv, SS, lsem.at[3])
    for copy in own:
        copy.start()

    barrier = pltpu.get_barrier_semaphore()

    def signal(dev):
        pl.semaphore_signal(barrier, inc=1, device_id=dev, device_id_type=MESH)

    @pl.when(is1)
    def _():
        @pl.when(c < LAST)
        def _():
            signal((p + 2, me))

        @pl.when(c > 0)
        def _():
            signal((p - 2, me))

        signal(pair)

    def greet(k, _):
        o = lax.rem(me + k, PEERS)

        @pl.when(k > 0)
        def _():
            signal((p, o))

        @pl.when(is0)
        def _():
            signal((p + 1, o))

        return 0

    lax.fori_loop(0, PEERS, greet, 0)
    CP[core, 0:2, :] = cd[...]
    CP[core, 2:4, :] = cu[...]
    Z[...] = jnp.zeros_like(Z)
    Z[0:2, :] = pm[...].astype(F32)
    Z[2:4, :] = pm[...].astype(F32)
    targets = Z[...].T.reshape(PEERS, 2, ROWS, 128)
    lane = lax.broadcasted_iota(jnp.int32, (PEERS, ROWS, 128), 2)
    PMS[...] = jnp.where(lane < 2, targets[:, 0], targets[:, 1]).reshape(PEERS * ROWS, 128)

    @pl.when(jnp.logical_and(is0, first))
    def _():
        for f in range(2):
            own[f].wait()
            DA[f] = dot(src[f].astype(BF16), A[0, f]).astype(BF16)

    ends = jnp.where(first, 0, 1) + jnp.where(last, 0, 1)
    far = PEERS + ends
    pl.semaphore_wait(barrier, PEERS - 1 + jnp.where(is1, far, 1))

    send_a = [to_pair(inv.at[f], A.at[core, f], S_A + f) for f in range(2)]
    got_a = [to_pair(inv.at[f], A.at[1 - core, f], S_A + f) for f in range(2)]
    send_cp = to_pair(CP.at[core], CP.at[core], S_CP)
    got_cp = to_pair(CP.at[core], CP.at[1 - core], S_CP)
    send_src = to_pair(src, SL, S_SRC)
    send_lift = to_pair(lift, LL.at[0], S_LIFT)
    ship_p = [to_pair(PP.at[f], PP.at[f], S_P + f) for f in range(2)]
    ship_q = [to_pair(QQ.at[f], QQ.at[f], S_Q + f) for f in range(2)]
    ship_ua = to_pair(UA, UA, S_UA)
    ship_da = [to_pair(DA.at[f], DA.at[f], S_DA + f) for f in range(2)]
    def part(k):
        return pl.ds(pl.multiple_of(k * ROWS, ROWS), ROWS)

    def to_owners(out, into, lane, target, to_self):
        def one(k, _):
            o = lax.rem(me + k, PEERS)
            remote(
                out.at[part(o)], into.at[me], osnd.at[lane], orcv.at[lane], (2 * c + target, o)
            ).start()
            return 0

        lax.fori_loop(0 if to_self else 1, PEERS, one, 0)
        if not to_self:
            into[me] = out[part(me), :]

    def several(ref, n, lane):
        some = ref.at[pl.ds(0, n)]
        return remote(some, some, osnd.at[lane], orcv.at[lane], pair)

    def send_targets():
        to_owners(PMS, PMR, 3, core, False)

    def build_maps():
        several(PMR, PEERS - 1, 3).wait()
        table = PMR[...].reshape(SHARE, 128)
        column = (lax.broadcasted_iota(jnp.int32, (SHARE, SHARE), 1) + me * SHARE).astype(F32)
        for q in range(4):
            ONE[q] = jnp.where(table[:, q : q + 1] == column, 1.0, 0.0).astype(BF16)

    def turned(ref):
        return ref[...].astype(F32).reshape(SHARE, 128).T.astype(BF16)

    def separator(x, swept):
        several(UPR, PEERS - x, 4 + x).wait_recv()
        updates = turned(UPR)
        gathered = jnp.zeros((RHS, SHARE), F32)
        for q in range(4):
            gathered += dot(updates[q * RHS : (q + 1) * RHS, :], ONE[q])
        RED[me] = (ssep[...] - gathered).astype(BF16)

        def spread(k):
            o = lax.rem(me + k, PEERS)
            return remote(RED.at[me], RED.at[me], rsnd.at[k], rrcv.at[k], (p, o))

        for k in range(1, PEERS):
            spread(k).start()
        own_sep.wait()
        total = jnp.zeros((RHS, SHARE), F32)
        for group in range(0, PEERS, GROUP):
            sources = [lax.rem(me + PEERS - k, PEERS) for k in range(group, group + GROUP)]
            for k, w in zip(range(group, group + GROUP), sources):
                if k:
                    remote(RED.at[w], RED.at[w], rsnd.at[k], rrcv.at[k], pair).wait_recv()
            for w in sources:
                total += dot(RED[w], SS[pl.ds(pl.multiple_of(w * SHARE, SHARE), SHARE), :])
        half = total.astype(BF16)
        for q in range(4):
            ZP[q * RHS : (q + 1) * RHS, :] = dot_t(half, ONE[q])
        PKS[...] = ZP[...].T.astype(BF16)
        to_owners(PKS, PKR, 6, x, False)
        sep_out[...] = total
        for copy in own_lower:
            copy.wait()
        if x == 0:
            ship_ua.wait_recv()
        several(PKR, PEERS - 1, 6).wait()
        picked = turned(PKR)
        for f in range(2):
            back = dot(picked[f * RHS : (f + 1) * RHS, :], LW[f, 0].reshape(SHARE, LEAF))
            back += dot(picked[(2 + f) * RHS : (3 + f) * RHS, :], LW[f, 1].reshape(SHARE, LEAF))
            leaf_out[f] = swept[f] - back
        for k in range(1, PEERS):
            spread(k).wait_send()

    @pl.when(is0)
    def _core0():
        @pl.when(first)
        def _():
            for copy in ship_da:
                copy.start()

        send_cp.start()
        send_src.start()
        send_a[0].start()
        send_a[1].start()
        send_targets()
        own_sep.start()
        for copy in own_lower:
            copy.start()
        got_cp.wait_recv()
        for x in range(2):
            CT[x] = CP[x].T
        for f in range(2):

            @pl.when(c > 0)
            def _():
                own[f].wait()

            got_a[f].wait_recv()

        @pl.when(c > DIRECT)
        def _():
            for f in range(2):

                @pl.loop(0, 4)
                def _(b):
                    rows = pl.ds(pl.multiple_of(b * 256, 256), 256)
                    left = (A[0, f, rows, :].astype(F32) * CP[1, f : f + 1, :]).astype(BF16)
                    PP[f, rows, :] = (dot(left, A[1, f]) * CT[0, rows, f : f + 1]).astype(BF16)
                    to_pair(PP.at[f, rows], PP.at[f, rows], S_P + f).start()

        send_lift.start()
        for f in range(2):

            @pl.loop(0, 4)
            def _(b):
                rows = pl.ds(pl.multiple_of(b * 256, 256), 256)
                base = jnp.where(last, PP[f, rows, :].astype(F32), A[1, f, rows, :].astype(F32))
                left = (base * CP[0, f + 2 : f + 3, :]).astype(BF16)
                scale = jnp.where(last, 1.0, CT[1, rows, f + 2 : f + 3])
                extra = jnp.where(last, CT[0, rows, f : f + 1], 0.0)
                full = dot(left, A[0, f]) * scale + extra * A[0, f, rows, :].astype(F32)
                QQ[f, rows, :] = full.astype(BF16)
                to_pair(QQ.at[f, rows], QQ.at[f, rows], S_Q + f).start()

        build_maps()
        separator(0, UA)
        for copy in (send_cp, send_src, *send_a, send_lift, *ship_q):
            copy.wait_send()

        @pl.when(c > DIRECT)
        def _():
            for copy in ship_p:
                copy.wait_send()

        @pl.when(first)
        def _():
            for copy in ship_da:
                copy.wait_send()

    def wave_of(w):
        return w // 2, slice(w % 2 * HALF, w % 2 * HALF + HALF)

    @pl.when(is1)
    def _core1():
        send_cp.start()
        send_a[0].start()
        send_a[1].start()
        send_targets()
        own_sep.start()
        own_lift.start()
        for copy in own_lower:
            copy.start()

        below = (p + 2, me)
        above = (p - 2, me)

        def down_wave(w, cols=slice(None)):
            f, rows = wave_of(w)
            return remote(TS.at[f, rows, cols], T.at[f, rows, cols], dsnd.at[w], drcv.at[w], below)

        def up_wave(w, cols=slice(None)):
            f, rows = wave_of(w)
            return remote(US.at[f, rows, cols], U.at[f, rows, cols], usnd.at[w], urcv.at[w], above)

        def coupled(x, f, k):
            return CP[x, pl.ds(f + k, 1), :]

        def each_wave(step):
            for w in range(WAVES):
                step(w)

        def solve(w, left, weight, extra, keep, half, copy_of):
            f, rows = wave_of(w)
            parts = [slice(j * CHUNK, (j + 1) * CHUNK) for j in range(CHUNKS)]
            outs = []
            for cols in parts:
                out = dot(left, weight[f, :, cols])
                outs.append(out if extra is None else out + extra[f, rows, cols])
            for cols, out in zip(parts, outs):
                half[f, rows, cols] = out.astype(BF16)
                if copy_of is not None:
                    copy_of(w, cols).start()
            for cols, out in zip(parts, outs):
                keep[f, rows, cols] = out

        got_cp.wait_recv()

        @pl.when(first)
        def _():
            T[...] = jnp.zeros_like(T)

            def step(w):
                f, rows = wave_of(w)
                if w % 2 == 0:
                    own[f].wait()
                    ship_da[f].wait_recv()
                loaded = src[f, rows, :] + coupled(1, f, 0) * DA[f, rows, :].astype(F32)
                solve(w, loaded.astype(BF16), A.at[1], None, DB, TS, down_wave)

            each_wave(step)
            send_src.wait_recv()
            for f in range(2):
                got_a[f].wait_recv()

        @pl.when(jnp.logical_and(c > 0, c <= DIRECT))
        def _():
            send_src.wait_recv()

            def step(w):
                f, rows = wave_of(w)
                if w % 2 == 0:
                    got_a[f].wait_recv()
                    own[f].wait()
                down_wave(w).wait_recv()
                loaded = SL[f, rows, :] + coupled(0, f, 0) * T[f, rows, :].astype(F32)
                middle = dot(loaded.astype(BF16), A[0, f])
                loaded = src[f, rows, :] + coupled(1, f, 0) * middle.astype(BF16).astype(F32)
                solve(w, loaded.astype(BF16), A.at[1], None, DB, TS, down_wave)

            each_wave(step)

        @pl.when(c <= DIRECT)
        def _():
            build_maps()

        @pl.when(c > DIRECT)
        def _():
            send_src.wait_recv()
            for f in range(2):
                got_a[f].wait_recv()
                own[f].wait()

            def alone(f, _):
                middle = dot(SL[f].astype(BF16), A[0, f])
                loaded = src[f] + coupled(1, f, 0) * middle.astype(BF16).astype(F32)
                out = dot(loaded.astype(BF16), A[1, f])
                DB[f] = out
                E[f] = out

                @pl.when(last)
                def _():
                    loaded = SL[f] + coupled(0, f, 2) * out.astype(BF16).astype(F32)
                    E[f] = dot(loaded.astype(BF16), A[0, f])

                return 0

            lax.fori_loop(0, 2, alone, 0)
            build_maps()

            def sweep(weight, keep, half, copy_of):
                def step(w):
                    f, rows = wave_of(w)
                    down_wave(w).wait_recv()
                    solve(w, T[f, rows, :], weight, E, keep, half, copy_of)

                each_wave(step)

            for f in range(2):
                ship_p[f].wait_recv()

            @pl.when(c < LAST)
            def _():
                sweep(PP, DB, TS, down_wave)

            @pl.when(last)
            def _():
                for f in range(2):
                    ship_q[f].wait_recv()
                sweep(QQ, UA, US, up_wave)

        @pl.when(c < LAST)
        def _():
            def before(f, _):
                loaded = (
                    SL[f]
                    + coupled(0, f, 0) * T[f].astype(F32)
                    + coupled(0, f, 2) * DB[f].astype(BF16).astype(F32)
                )
                G[f] = dot(loaded.astype(BF16), A[0, f])
                return 0

            lax.fori_loop(0, 2, before, 0)
            for f in range(2):
                ship_q[f].wait_recv()

            def step(copy_of, w):
                f, rows = wave_of(w)
                up_wave(w).wait_recv()
                solve(w, U[f, rows, :], QQ, G, UA, US, copy_of)

            @pl.when(first)
            def _():
                each_wave(functools.partial(step, None))

            @pl.when(c > 0)
            def _():
                each_wave(functools.partial(step, up_wave))

        def lifted(x, half):
            for f in range(2):
                Z[f * RHS : (f + 1) * RHS, :] = dot(half[f], LL[x, f])
            rows = Z[0 : 2 * RHS, :].T.reshape(PEERS, 2, ROWS, 2 * RHS)
            packed = jnp.concatenate([rows[:, 0], rows[:, 1]], axis=-1)
            UPS[x] = packed.reshape(SHARE, 128).astype(BF16)
            to_owners(UPS.at[x], UPR, 4 + x, x, x == 0)

        send_lift.wait_recv()
        own_lift.wait()
        lifted(0, US)
        ship_ua.start()

        @pl.when(last)
        def _():
            def rest(f, _):
                UB[f] = DB[f] + dot(T[f], PP[f])
                return 0

            lax.fori_loop(0, 2, rest, 0)

        @pl.when(c < LAST)
        def _():
            def rest(f, _):
                loaded = coupled(1, f, 2) * U[f].astype(F32)
                UB[f] = DB[f] + dot(loaded.astype(BF16), A[1, f])
                return 0

            lax.fori_loop(0, 2, rest, 0)

        for f in range(2):
            DA[f] = UB[f].astype(BF16)
        lifted(1, DA)
        separator(1, UB)

        for copy in (send_cp, *send_a, ship_ua):
            copy.wait_send()
        several(UPR, PEERS, 4).wait_send()
        several(UPR, PEERS - 1, 5).wait_send()

        @pl.when(c < LAST)
        def _():
            each_wave(lambda w: down_wave(w).wait_send())

        @pl.when(c > 0)
        def _():
            each_wave(lambda w: up_wave(w).wait_send())


def local(source_leaf, source_sep, leaf_inverse, lift, lower, sep_inverse, parent_map, couple_down, couple_up):
    vmem = pl.BlockSpec(memory_space=pltpu.VMEM)
    hbm = pl.BlockSpec(memory_space=pl.ANY)
    trace = (2, RHS, LEAF)
    leaf, sep = pl.pallas_call(
        kernel,
        out_shape=(
            jax.ShapeDtypeStruct(trace, F32),
            jax.ShapeDtypeStruct((RHS, SHARE), F32),
        ),
        in_specs=[vmem, vmem, hbm, hbm, hbm, hbm, vmem, vmem, vmem],
        out_specs=(vmem, vmem),
        scratch_shapes=[
            pltpu.VMEM((2, 2, LEAF, LEAF), BF16),
            pltpu.VMEM((2, LEAF, LEAF), BF16),
            pltpu.VMEM((2, LEAF, LEAF), BF16),
            pltpu.VMEM((2, 2, LEAF, UPD), BF16),
            pltpu.VMEM((2, 2, PEERS, ROWS, LEAF), BF16),
            pltpu.VMEM((PEERS * SHARE, SHARE), BF16),
            pltpu.VMEM(trace, F32),
            pltpu.VMEM((2, 8, LEAF), F32),
            pltpu.VMEM((2, LEAF, 8), F32),
            *[pltpu.VMEM(trace, BF16) for _ in range(5)],
            *[pltpu.VMEM(trace, F32) for _ in range(5)],
            pltpu.VMEM((128, UPD), F32),
            pltpu.VMEM((128, SHARE), F32),
            pltpu.VMEM((SHARE, 128), F32),
            pltpu.VMEM((PEERS, ROWS, 128), F32),
            pltpu.VMEM((2, SHARE, 128), BF16),
            pltpu.VMEM((PEERS, ROWS, 128), BF16),
            pltpu.VMEM((4, SHARE, SHARE), BF16),
            pltpu.VMEM((PEERS, RHS, SHARE), BF16),
            pltpu.VMEM((SHARE, 128), BF16),
            pltpu.VMEM((PEERS, ROWS, 128), BF16),
            pltpu.SemaphoreType.DMA((8,)),
            pltpu.SemaphoreType.DMA((12,)),
            pltpu.SemaphoreType.DMA((12,)),
            *[pltpu.SemaphoreType.DMA((WAVES,)) for _ in range(4)],
            pltpu.SemaphoreType.DMA((8,)),
            pltpu.SemaphoreType.DMA((8,)),
            pltpu.SemaphoreType.DMA((PEERS,)),
            pltpu.SemaphoreType.DMA((PEERS,)),
        ],
        compiler_params=pltpu.CompilerParams(
            collective_id=0, has_side_effects=True, vmem_limit_bytes=56 * 1024 * 1024
        ),
        name="sweep",
    )(
        source_leaf[0], source_sep[0], leaf_inverse[0], lift[0], lower.reshape(2, PEERS, 2, ROWS, LEAF),
        sep_inverse[0], parent_map[0], couple_down[0], couple_up[0],
    )
    return leaf[None], sep[None]


def solution(mesh):
    return jax.shard_map(
        local,
        mesh=mesh,
        in_specs=(
            P("panel", "front", None, None),
            P("panel", None, "front"),
            P("panel", "front", None, None),
            P("panel", "front", None, None),
            P("panel", "front", None, None),
            P("panel", None, "front"),
            P("panel", "front", None),
            P("panel", "front", None),
            P("panel", "front", None),
        ),
        out_specs=(P("panel", "front", None, None), P("panel", None, "front")),
        check_vma=False,
    )
```

time: 92.7 us -> 81.7 us (0.88)
  Pallas kernels: 88.8 us -> 77.8 us
    pallas_call x1, Pallas kernels: 88.8 us -> 77.8 us  [local(): pl.pallas_call(kernel, out_shape=(jax.ShapeDtypeStruct(trace, F32), jax.S...]
where the time goes in v2:
time: 81.7 us; the launch traced here: 81.5 us
  Pallas kernels  77.8 us (95%)
  local copies, waits for them, and re-layouts  3.05 us (4%)
    pallas_call x1, Pallas kernels, local(): pl.pallas_call(kernel, out_shape=(jax.ShapeDtypeStruct(trace, F32), jax.S...  77.8 us
    unnamed x2, local copies, waits for them, and re-layouts  3.05 us

profile of v2, /device:TPU:1, one launch (start us, length us, event | category | flops | bytes accessed | tf_op | source)
XLA Modules:
  0.0 81.5 jit_solution(10112714599872368673)
XLA Ops:
  0.6 77.8 %sweep.1 = (f32[2,32,1024]{2,1,0:T(8,128)}, f32[32,256]{1,0:T(8,128)}) custom-call(f32[2,32,1024]{2,1,0:T(8,128)} %bitcast.15, f32[32,256]{1,0:T(8,128)} %bitcast.17, bf16[2,1024,1024]{2,1,0:T(8,128)(2,1)} %bitcast.11, bf16[2,1024,512]{2,1,0:T(8,128)(2,1)} %bitcast.12, bf16[2,16,2,16,1024]{4,3,2,1,0:T(8,128)(2,1)} %bitcast.13, bf16[4096,256]{1,0:T(8,128)(2,1)} %bitcast.14, ...), custom_call_target="tpu_custom_call" | custom-call | tf_op jit(solution)/shard_map/sweep/pallas_call | solution.py:486
  78.5 1.7 %copy.13 = f32[1,2,32,1024]{3,2,1,0:T(8,128)} copy(f32[1,2,32,1024]{3,2,1,0:T(8,128)} %bitcast.16) | data formatting | bytes 524288
  80.1 1.4 %copy.14 = f32[1,32,256]{2,1,0:T(8,128)} copy(f32[1,32,256]{2,1,0:T(8,128)} %bitcast.18) | data formatting | bytes 65536

commit v3 on v2

--- a/solution.py
+++ b/solution.py
@@ -1,5 +1,3 @@
-import functools
-
 import jax
 import jax.numpy as jnp
 from jax import lax
@@ -121,8 +119,20 @@
     far = PEERS + ends
     pl.semaphore_wait(barrier, PEERS - 1 + jnp.where(is1, far, 1))
 
-    send_a = [to_pair(inv.at[f], A.at[core, f], S_A + f) for f in range(2)]
-    got_a = [to_pair(inv.at[f], A.at[1 - core, f], S_A + f) for f in range(2)]
+    send_a = [to_pair(A.at[core, f], A.at[core, f], S_A + f) for f in range(2)]
+    got_a = [to_pair(A.at[core, f], A.at[1 - core, f], S_A + f) for f in range(2)]
+
+    def give_a():
+        for f in range(2):
+
+            @pl.when(jnp.logical_or(is1, c > 0))
+            def _():
+                own[f].wait()
+
+            for half in range(2):
+                rows = pl.ds(half * 512, 512)
+                to_pair(A.at[core, f, rows], A.at[core, f, rows], S_A + f).start()
+
     send_cp = to_pair(CP.at[core], CP.at[core], S_CP)
     got_cp = to_pair(CP.at[core], CP.at[1 - core], S_CP)
     send_src = to_pair(src, SL, S_SRC)
@@ -214,21 +224,12 @@
 
         send_cp.start()
         send_src.start()
-        send_a[0].start()
-        send_a[1].start()
+        give_a()
         send_targets()
-        own_sep.start()
-        for copy in own_lower:
-            copy.start()
         got_cp.wait_recv()
         for x in range(2):
             CT[x] = CP[x].T
         for f in range(2):
-
-            @pl.when(c > 0)
-            def _():
-                own[f].wait()
-
             got_a[f].wait_recv()
 
         @pl.when(c > DIRECT)
@@ -242,7 +243,6 @@
                     PP[f, rows, :] = (dot(left, A[1, f]) * CT[0, rows, f : f + 1]).astype(BF16)
                     to_pair(PP.at[f, rows], PP.at[f, rows], S_P + f).start()
 
-        send_lift.start()
         for f in range(2):
 
             @pl.loop(0, 4)
@@ -256,6 +256,10 @@
                 QQ[f, rows, :] = full.astype(BF16)
                 to_pair(QQ.at[f, rows], QQ.at[f, rows], S_Q + f).start()
 
+        send_lift.start()
+        own_sep.start()
+        for copy in own_lower:
+            copy.start()
         build_maps()
         separator(0, UA)
         for copy in (send_cp, send_src, *send_a, send_lift, *ship_q):
@@ -271,14 +275,10 @@
             for copy in ship_da:
                 copy.wait_send()
 
-    def wave_of(w):
-        return w // 2, slice(w % 2 * HALF, w % 2 * HALF + HALF)
-
     @pl.when(is1)
     def _core1():
         send_cp.start()
-        send_a[0].start()
-        send_a[1].start()
+        give_a()
         send_targets()
         own_sep.start()
         own_lift.start()
@@ -288,34 +288,48 @@
         below = (p + 2, me)
         above = (p - 2, me)
 
-        def down_wave(w, cols=slice(None)):
-            f, rows = wave_of(w)
-            return remote(TS.at[f, rows, cols], T.at[f, rows, cols], dsnd.at[w], drcv.at[w], below)
-
-        def up_wave(w, cols=slice(None)):
-            f, rows = wave_of(w)
-            return remote(US.at[f, rows, cols], U.at[f, rows, cols], usnd.at[w], urcv.at[w], above)
+        def down_wave(f, g, cols=slice(None)):
+            rows, k = half_rows(g), 2 * f + g
+            return remote(TS.at[f, rows, cols], T.at[f, rows, cols], dsnd.at[k], drcv.at[k], below)
+
+        def up_wave(f, g, cols=slice(None)):
+            rows, k = half_rows(g), 2 * f + g
+            return remote(US.at[f, rows, cols], U.at[f, rows, cols], usnd.at[k], urcv.at[k], above)
+
+        def half_rows(g):
+            return pl.ds(pl.multiple_of(g * HALF, HALF), HALF)
 
         def coupled(x, f, k):
             return CP[x, pl.ds(f + k, 1), :]
 
-        def each_wave(step):
+        def each_wave(act):
             for w in range(WAVES):
-                step(w)
-
-        def solve(w, left, weight, extra, keep, half, copy_of):
-            f, rows = wave_of(w)
-            parts = [slice(j * CHUNK, (j + 1) * CHUNK) for j in range(CHUNKS)]
-            outs = []
-            for cols in parts:
-                out = dot(left, weight[f, :, cols])
-                outs.append(out if extra is None else out + extra[f, rows, cols])
-            for cols, out in zip(parts, outs):
-                half[f, rows, cols] = out.astype(BF16)
-                if copy_of is not None:
-                    copy_of(w, cols).start()
-            for cols, out in zip(parts, outs):
-                keep[f, rows, cols] = out
+                act(w // 2, w % 2)
+
+        def waves(ready, left_of, weight, extra, keep, half, copy_of):
+            def turn(i, _):
+                w = i
+                g = lax.rem(w, 2)
+                f = w // 2
+                rows = half_rows(g)
+
+                ready(f, g)
+                left = left_of(f, rows)
+                parts = [slice(j * CHUNK, (j + 1) * CHUNK) for j in range(CHUNKS)]
+                outs = []
+                for cols in parts:
+                    out = dot(left, weight[f, :, cols])
+                    outs.append(out if extra is None else out + extra[f, rows, cols])
+                for cols, out in zip(parts, outs):
+                    half[f, rows, cols] = out.astype(BF16)
+                    if copy_of is not None:
+                        copy_of(f, g, cols).start()
+
+                for cols, out in zip(parts, outs):
+                    keep[f, rows, cols] = out
+                return 0
+
+            lax.fori_loop(0, WAVES, turn, 0)
 
         got_cp.wait_recv()
 
@@ -323,35 +337,40 @@
         def _():
             T[...] = jnp.zeros_like(T)
 
-            def step(w):
-                f, rows = wave_of(w)
-                if w % 2 == 0:
-                    own[f].wait()
-                    ship_da[f].wait_recv()
+            def ready(f, g):
+                @pl.when(g == 0)
+                def _():
+                    to_pair(DA.at[f], DA.at[f], S_DA + f).wait_recv()
+
+            def left_of(f, rows):
                 loaded = src[f, rows, :] + coupled(1, f, 0) * DA[f, rows, :].astype(F32)
-                solve(w, loaded.astype(BF16), A.at[1], None, DB, TS, down_wave)
-
-            each_wave(step)
+                return loaded.astype(BF16)
+
+            waves(ready, left_of, A.at[1], None, DB, TS, down_wave)
             send_src.wait_recv()
             for f in range(2):
                 got_a[f].wait_recv()
 
         @pl.when(jnp.logical_and(c > 0, c <= DIRECT))
         def _():
-            send_src.wait_recv()
-
-            def step(w):
-                f, rows = wave_of(w)
-                if w % 2 == 0:
-                    got_a[f].wait_recv()
-                    own[f].wait()
-                down_wave(w).wait_recv()
+            def ready(f, g):
+                @pl.when(f + g == 0)
+                def _():
+                    send_src.wait_recv()
+
+                @pl.when(g == 0)
+                def _():
+                    to_pair(A.at[core, f], A.at[1 - core, f], S_A + f).wait_recv()
+
+                down_wave(f, g).wait_recv()
+
+            def left_of(f, rows):
                 loaded = SL[f, rows, :] + coupled(0, f, 0) * T[f, rows, :].astype(F32)
                 middle = dot(loaded.astype(BF16), A[0, f])
                 loaded = src[f, rows, :] + coupled(1, f, 0) * middle.astype(BF16).astype(F32)
-                solve(w, loaded.astype(BF16), A.at[1], None, DB, TS, down_wave)
-
-            each_wave(step)
+                return loaded.astype(BF16)
+
+            waves(ready, left_of, A.at[1], None, DB, TS, down_wave)
 
         @pl.when(c <= DIRECT)
         def _():
@@ -362,7 +381,6 @@
             send_src.wait_recv()
             for f in range(2):
                 got_a[f].wait_recv()
-                own[f].wait()
 
             def alone(f, _):
                 middle = dot(SL[f].astype(BF16), A[0, f])
@@ -381,26 +399,25 @@
             lax.fori_loop(0, 2, alone, 0)
             build_maps()
 
-            def sweep(weight, keep, half, copy_of):
-                def step(w):
-                    f, rows = wave_of(w)
-                    down_wave(w).wait_recv()
-                    solve(w, T[f, rows, :], weight, E, keep, half, copy_of)
-
-                each_wave(step)
-
-            for f in range(2):
-                ship_p[f].wait_recv()
+            def sweep(ship, weight, keep, half, copy_of):
+                def ready(f, g):
+                    @pl.when(g == 0)
+                    def _():
+                        to_pair(weight.at[f], weight.at[f], ship + f).wait_recv()
+
+                    down_wave(f, g).wait_recv()
+
+                waves(ready, lambda f, rows: T[f, rows, :], weight, E, keep, half, copy_of)
 
             @pl.when(c < LAST)
             def _():
-                sweep(PP, DB, TS, down_wave)
+                sweep(S_P, PP, DB, TS, down_wave)
 
             @pl.when(last)
             def _():
+                sweep(S_Q, QQ, UA, US, up_wave)
                 for f in range(2):
-                    ship_q[f].wait_recv()
-                sweep(QQ, UA, US, up_wave)
+                    ship_p[f].wait_recv()
 
         @pl.when(c < LAST)
         def _():
@@ -414,21 +431,24 @@
                 return 0
 
             lax.fori_loop(0, 2, before, 0)
-            for f in range(2):
-                ship_q[f].wait_recv()
-
-            def step(copy_of, w):
-                f, rows = wave_of(w)
-                up_wave(w).wait_recv()
-                solve(w, U[f, rows, :], QQ, G, UA, US, copy_of)
+
+            def ready(f, g):
+                @pl.when(g == 0)
+                def _():
+                    to_pair(QQ.at[f], QQ.at[f], S_Q + f).wait_recv()
+
+                up_wave(f, g).wait_recv()
+
+            def left_of(f, rows):
+                return U[f, rows, :]
 
             @pl.when(first)
             def _():
-                each_wave(functools.partial(step, None))
+                waves(ready, left_of, QQ, G, UA, US, None)
 
             @pl.when(c > 0)
             def _():
-                each_wave(functools.partial(step, up_wave))
+                waves(ready, left_of, QQ, G, UA, US, up_wave)
 
         def lifted(x, half):
             for f in range(2):
@@ -472,11 +492,16 @@
 
         @pl.when(c < LAST)
         def _():
-            each_wave(lambda w: down_wave(w).wait_send())
+            each_wave(lambda f, g: down_wave(f, g).wait_send())
 
         @pl.when(c > 0)
         def _():
-            each_wave(lambda w: up_wave(w).wait_send())
+            each_wave(lambda f, g: up_wave(f, g).wait_send())
+
+
+def hand_over(leaf, sep, leaf_out, sep_out):
+    leaf_out[...] = leaf[...]
+    sep_out[...] = sep[...]
 
 
 def local(source_leaf, source_sep, leaf_inverse, lift, lower, sep_inverse, parent_map, couple_down, couple_up):
@@ -530,6 +555,13 @@
         source_leaf[0], source_sep[0], leaf_inverse[0], lift[0], lower.reshape(2, PEERS, 2, ROWS, LEAF),
         sep_inverse[0], parent_map[0], couple_down[0], couple_up[0],
     )
+    leaf, sep = pl.pallas_call(
+        hand_over,
+        out_shape=(jax.ShapeDtypeStruct(trace, F32), jax.ShapeDtypeStruct((RHS, SHARE), F32)),
+        in_specs=[vmem, vmem],
+        out_specs=(vmem, vmem),
+        name="hand_over",
+    )(leaf, sep)
     return leaf[None], sep[None]
 
 

time: 81.7 us -> 77.6 us (0.950)
  local copies, waits for them, and re-layouts: 3.05 us -> 0 us
  Pallas kernels: 77.8 us -> 76.8 us
    unnamed x2 -> x0, local copies, waits for them, and re-layouts: 3.05 us -> none
    pallas_call x1, Pallas kernels: 77.8 us -> 75.1 us  [local(): pl.pallas_call(kernel, out_shape=(jax.ShapeDtypeStruct(trace, F32), jax.S...]
    pallas_call x0 -> x1, Pallas kernels: none -> 1.68 us  [local(): pl.pallas_call(hand_over, out_shape=(jax.ShapeDtypeStruct(trace, F32), ja...]
where the time goes in v3:
time: 77.6 us; the launch traced here: 77.5 us
  Pallas kernels  76.8 us (99%)
    pallas_call x1, Pallas kernels, local(): pl.pallas_call(kernel, out_shape=(jax.ShapeDtypeStruct(trace, F32), jax.S...  75.1 us
    pallas_call x1, Pallas kernels, local(): pl.pallas_call(hand_over, out_shape=(jax.ShapeDtypeStruct(trace, F32), ja...  1.68 us

profile of v3, /device:TPU:1, one launch (start us, length us, event | category | flops | bytes accessed | tf_op | source)
XLA Modules:
  0.0 77.5 jit_solution(11175083640749424677)
XLA Ops:
  0.6 75.1 %sweep.1 = (f32[2,32,1024]{2,1,0:T(8,128)}, f32[32,256]{1,0:T(8,128)}) custom-call(f32[2,32,1024]{2,1,0:T(8,128)} %bitcast.15, f32[32,256]{1,0:T(8,128)} %bitcast.16, bf16[2,1024,1024]{2,1,0:T(8,128)(2,1)} %bitcast.11, bf16[2,1024,512]{2,1,0:T(8,128)(2,1)} %bitcast.12, bf16[2,16,2,16,1024]{4,3,2,1,0:T(8,128)(2,1)} %bitcast.13, bf16[4096,256]{1,0:T(8,128)(2,1)} %bitcast.14, ...), custom_call_target="tpu_custom_call" | custom-call | tf_op jit(solution)/shard_map/sweep/pallas_call | solution.py:511
  75.8 1.7 %hand_over.1 = (f32[2,32,1024]{2,1,0:T(8,128)}, f32[32,256]{1,0:T(8,128)}) custom-call(f32[2,32,1024]{2,1,0:T(8,128)} %get-tuple-element.6.leaf, f32[32,256]{1,0:T(8,128)} %get-tuple-element.7.sep), custom_call_target="tpu_custom_call" | custom-call | tf_op jit(solution)/shard_map/hand_over/pallas_call | solution.py:558

commit v4 on v3

--- a/solution.py
+++ b/solution.py
@@ -144,15 +144,20 @@
     def part(k):
         return pl.ds(pl.multiple_of(k * ROWS, ROWS), ROWS)
 
+    def flipped(v, bits):
+        return (v, v + 1 - 2 * lax.rem(v, 2), lax.rem(v + 2, 4), 3 - v)[bits]
+
+    def across(k):
+        return 4 * flipped(me // 4, k // 4) + flipped(lax.rem(me, 4), k % 4)
+
+    far_first = range(PEERS - 1, 0, -1)
+
     def to_owners(out, into, lane, target, to_self):
-        def one(k, _):
-            o = lax.rem(me + k, PEERS)
+        for k in (*far_first, *([0] if to_self else [])):
+            o = across(k)
             remote(
                 out.at[part(o)], into.at[me], osnd.at[lane], orcv.at[lane], (2 * c + target, o)
             ).start()
-            return 0
-
-        lax.fori_loop(0 if to_self else 1, PEERS, one, 0)
         if not to_self:
             into[me] = out[part(me), :]
 
@@ -182,15 +187,15 @@
         RED[me] = (ssep[...] - gathered).astype(BF16)
 
         def spread(k):
-            o = lax.rem(me + k, PEERS)
+            o = across(k)
             return remote(RED.at[me], RED.at[me], rsnd.at[k], rrcv.at[k], (p, o))
 
-        for k in range(1, PEERS):
+        for k in far_first:
             spread(k).start()
         own_sep.wait()
         total = jnp.zeros((RHS, SHARE), F32)
         for group in range(0, PEERS, GROUP):
-            sources = [lax.rem(me + PEERS - k, PEERS) for k in range(group, group + GROUP)]
+            sources = [across(k) for k in range(group, group + GROUP)]
             for k, w in zip(range(group, group + GROUP), sources):
                 if k:
                     remote(RED.at[w], RED.at[w], rsnd.at[k], rrcv.at[k], pair).wait_recv()
@@ -499,9 +504,15 @@
             each_wave(lambda f, g: up_wave(f, g).wait_send())
 
 
-def hand_over(leaf, sep, leaf_out, sep_out):
-    leaf_out[...] = leaf[...]
-    sep_out[...] = sep[...]
+def hand_over(leaf, sep, leaf_out, sep_out, sem):
+    copies = [
+        pltpu.make_async_copy(leaf, leaf_out, sem.at[0]),
+        pltpu.make_async_copy(sep, sep_out, sem.at[1]),
+    ]
+    for copy in copies:
+        copy.start()
+    for copy in copies:
+        copy.wait()
 
 
 def local(source_leaf, source_sep, leaf_inverse, lift, lower, sep_inverse, parent_map, couple_down, couple_up):
@@ -510,10 +521,7 @@
     trace = (2, RHS, LEAF)
     leaf, sep = pl.pallas_call(
         kernel,
-        out_shape=(
-            jax.ShapeDtypeStruct(trace, F32),
-            jax.ShapeDtypeStruct((RHS, SHARE), F32),
-        ),
+        out_shape=(pltpu.VMEM(trace, F32), pltpu.VMEM((RHS, SHARE), F32)),
         in_specs=[vmem, vmem, hbm, hbm, hbm, hbm, vmem, vmem, vmem],
         out_specs=(vmem, vmem),
         scratch_shapes=[
@@ -558,10 +566,14 @@
     leaf, sep = pl.pallas_call(
         hand_over,
         out_shape=(jax.ShapeDtypeStruct(trace, F32), jax.ShapeDtypeStruct((RHS, SHARE), F32)),
-        in_specs=[vmem, vmem],
-        out_specs=(vmem, vmem),
+        in_specs=[hbm, hbm],
+        out_specs=(hbm, hbm),
+        scratch_shapes=[pltpu.SemaphoreType.DMA((2,))],
         name="hand_over",
-    )(leaf, sep)
+    )(
+        pltpu.with_memory_space_constraint(leaf, pltpu.VMEM),
+        pltpu.with_memory_space_constraint(sep, pltpu.VMEM),
+    )
     return leaf[None], sep[None]
 
 

time: 77.6 us -> 76 us (0.979)
  Pallas kernels: 76.8 us -> 75.3 us
    pallas_call x1, Pallas kernels: 1.68 us -> 0.72 us  [local(): pl.pallas_call(hand_over, out_shape=(jax.ShapeDtypeStruct(trace, F32), ja...]
where the time goes in v4:
time: 76 us; the launch traced here: 75.9 us
  Pallas kernels  75.3 us (99%)
    pallas_call x1, Pallas kernels, local(): pl.pallas_call(kernel, out_shape=(pltpu.VMEM(trace, F32), pltpu.VMEM((RHS...  74.6 us

profile of v4, /device:TPU:1, one launch (start us, length us, event | category | flops | bytes accessed | tf_op | source)
XLA Modules:
  0.0 75.9 jit_solution(13852754915971228975)
XLA Ops:
  0.6 74.6 %sweep.1 = (f32[2,32,1024]{2,1,0:T(8,128)S(1)}, f32[32,256]{1,0:T(8,128)S(1)}) custom-call(f32[2,32,1024]{2,1,0:T(8,128)} %bitcast.15, f32[32,256]{1,0:T(8,128)} %bitcast.16, bf16[2,1024,1024]{2,1,0:T(8,128)(2,1)} %bitcast.11, bf16[2,1024,512]{2,1,0:T(8,128)(2,1)} %bitcast.12, bf16[2,16,2,16,1024]{4,3,2,1,0:T(8,128)(2,1)} %bitcast.13, ...), custom_call_target="tpu_custom_call" | custom-call | tf_op jit(solution)/shard_map/sweep/pallas_call | solution.py:522
  75.2 0.7 hand_over.1

commit v5 on v4

--- a/solution.py
+++ b/solution.py
@@ -49,6 +49,7 @@
     is0 = core == 0
     is1 = core == 1
     first = c == 0
+    second = c == 1
     last = c == LAST
     def remote(s, d, ss, rs, dev):
         return pltpu.make_async_remote_copy(
@@ -86,6 +87,10 @@
 
         signal(pair)
 
+    @pl.when(jnp.logical_and(is0, second))
+    def _():
+        signal((p - 1, me))
+
     def greet(k, _):
         o = lax.rem(me + k, PEERS)
 
@@ -115,12 +120,17 @@
             own[f].wait()
             DA[f] = dot(src[f].astype(BF16), A[0, f]).astype(BF16)
 
-    ends = jnp.where(first, 0, 1) + jnp.where(last, 0, 1)
+    ends = 1 + jnp.where(last, 0, 1)
     far = PEERS + ends
     pl.semaphore_wait(barrier, PEERS - 1 + jnp.where(is1, far, 1))
 
     send_a = [to_pair(A.at[core, f], A.at[core, f], S_A + f) for f in range(2)]
     got_a = [to_pair(A.at[core, f], A.at[1 - core, f], S_A + f) for f in range(2)]
+
+    def give_front(f):
+        for half in range(2):
+            rows = pl.ds(half * 512, 512)
+            to_pair(A.at[core, f, rows], A.at[core, f, rows], S_A + f).start()
 
     def give_a():
         for f in range(2):
@@ -129,9 +139,13 @@
             def _():
                 own[f].wait()
 
-            for half in range(2):
-                rows = pl.ds(half * 512, 512)
-                to_pair(A.at[core, f, rows], A.at[core, f, rows], S_A + f).start()
+            if f == 0:
+                give_front(0)
+            else:
+
+                @pl.when(jnp.logical_or(is1, jnp.logical_not(second)))
+                def _():
+                    give_front(1)
 
     send_cp = to_pair(CP.at[core], CP.at[core], S_CP)
     got_cp = to_pair(CP.at[core], CP.at[1 - core], S_CP)
@@ -141,6 +155,14 @@
     ship_q = [to_pair(QQ.at[f], QQ.at[f], S_Q + f) for f in range(2)]
     ship_ua = to_pair(UA, UA, S_UA)
     ship_da = [to_pair(DA.at[f], DA.at[f], S_DA + f) for f in range(2)]
+    def side_wave(g, cols=slice(None)):
+        rows = pl.ds(pl.multiple_of(g * HALF, HALF), HALF)
+        return remote(TS.at[1, rows, cols], T.at[1, rows, cols], osnd.at[g], orcv.at[g], (p + 1, me))
+
+    def ship_middle(g):
+        rows = pl.ds(g * HALF, HALF)
+        return to_pair(DA.at[1, rows], DA.at[1, rows], S_DA + g)
+
     def part(k):
         return pl.ds(pl.multiple_of(k * ROWS, ROWS), ROWS)
 
@@ -231,6 +253,16 @@
         send_src.start()
         give_a()
         send_targets()
+        @pl.when(second)
+        def _():
+            for g in range(2):
+                rows = slice(g * HALF, (g + 1) * HALF)
+                side_wave(g).wait_recv()
+                loaded = src[1, rows, :] + CP[0, 1:2, :] * T[1, rows, :].astype(F32)
+                DA[1, rows, :] = dot(loaded.astype(BF16), A[0, 1]).astype(BF16)
+                ship_middle(g).start()
+            give_front(1)
+
         got_cp.wait_recv()
         for x in range(2):
             CT[x] = CP[x].T
@@ -280,6 +312,11 @@
             for copy in ship_da:
                 copy.wait_send()
 
+        @pl.when(second)
+        def _():
+            for g in range(2):
+                ship_middle(g).wait_send()
+
     @pl.when(is1)
     def _core1():
         send_cp.start()
@@ -301,6 +338,12 @@
             rows, k = half_rows(g), 2 * f + g
             return remote(US.at[f, rows, cols], U.at[f, rows, cols], usnd.at[k], urcv.at[k], above)
 
+        def send_down(f, g, cols):
+            down_wave(f, g, cols).start()
+
+        def send_up(f, g, cols):
+            up_wave(f, g, cols).start()
+
         def half_rows(g):
             return pl.ds(pl.multiple_of(g * HALF, HALF), HALF)
 
@@ -311,7 +354,7 @@
             for w in range(WAVES):
                 act(w // 2, w % 2)
 
-        def waves(ready, left_of, weight, extra, keep, half, copy_of):
+        def waves(ready, left_of, weight, extra, keep, half, copy_of, begin=0, end=WAVES):
             def turn(i, _):
                 w = i
                 g = lax.rem(w, 2)
@@ -328,13 +371,17 @@
                 for cols, out in zip(parts, outs):
                     half[f, rows, cols] = out.astype(BF16)
                     if copy_of is not None:
-                        copy_of(f, g, cols).start()
+                        copy_of(f, g, cols)
 
                 for cols, out in zip(parts, outs):
                     keep[f, rows, cols] = out
                 return 0
 
-            lax.fori_loop(0, WAVES, turn, 0)
+            lax.fori_loop(begin, end, turn, 0)
+
+        def left_of_middle(f, rows):
+            loaded = src[f, rows, :] + coupled(1, f, 0) * DA[f, rows, :].astype(F32)
+            return loaded.astype(BF16)
 
         got_cp.wait_recv()
 
@@ -347,11 +394,14 @@
                 def _():
                     to_pair(DA.at[f], DA.at[f], S_DA + f).wait_recv()
 
-            def left_of(f, rows):
-                loaded = src[f, rows, :] + coupled(1, f, 0) * DA[f, rows, :].astype(F32)
-                return loaded.astype(BF16)
-
-            waves(ready, left_of, A.at[1], None, DB, TS, down_wave)
+            def send_first(f, g, cols):
+                @pl.when(f == 1)
+                def _():
+                    side_wave(g, cols).start()
+
+                send_down(f, g, cols)
+
+            waves(ready, left_of_middle, A.at[1], None, DB, TS, send_first)
             send_src.wait_recv()
             for f in range(2):
                 got_a[f].wait_recv()
@@ -375,7 +425,22 @@
                 loaded = src[f, rows, :] + coupled(1, f, 0) * middle.astype(BF16).astype(F32)
                 return loaded.astype(BF16)
 
-            waves(ready, left_of, A.at[1], None, DB, TS, down_wave)
+            @pl.when(second)
+            def _():
+                waves(ready, left_of, A.at[1], None, DB, TS, send_down, 0, 2)
+
+                def ready_middle(f, g):
+                    to_pair(DA.at[1, half_rows(g)], DA.at[1, half_rows(g)], S_DA + g).wait_recv()
+
+                waves(ready_middle, left_of_middle, A.at[1], None, DB, TS, send_down, 2, 4)
+                got_a[1].wait_recv()
+                for g in range(2):
+                    down_wave(1, g).wait_recv()
+
+            @pl.when(c > 1)
+            def _():
+                waves(ready, left_of, A.at[1], None, DB, TS, send_down)
+
 
         @pl.when(c <= DIRECT)
         def _():
@@ -416,11 +481,11 @@
 
             @pl.when(c < LAST)
             def _():
-                sweep(S_P, PP, DB, TS, down_wave)
+                sweep(S_P, PP, DB, TS, send_down)
 
             @pl.when(last)
             def _():
-                sweep(S_Q, QQ, UA, US, up_wave)
+                sweep(S_Q, QQ, UA, US, send_up)
                 for f in range(2):
                     ship_p[f].wait_recv()
 
@@ -453,7 +518,7 @@
 
             @pl.when(c > 0)
             def _():
-                waves(ready, left_of, QQ, G, UA, US, up_wave)
+                waves(ready, left_of, QQ, G, UA, US, send_up)
 
         def lifted(x, half):
             for f in range(2):
@@ -498,6 +563,11 @@
         @pl.when(c < LAST)
         def _():
             each_wave(lambda f, g: down_wave(f, g).wait_send())
+
+        @pl.when(first)
+        def _():
+            for g in range(2):
+                side_wave(g).wait_send()
 
         @pl.when(c > 0)
         def _():

time: 76 us -> 74.8 us (0.984)
  Pallas kernels: 75.3 us -> 74.1 us
    pallas_call x1, Pallas kernels: 74.6 us -> 73.4 us  [local(): pl.pallas_call(kernel, out_shape=(pltpu.VMEM(trace, F32), pltpu.VMEM((RHS...]
where the time goes in v5:
time: 74.8 us; the launch traced here: 74.7 us
  Pallas kernels  74.1 us (99%)
    pallas_call x1, Pallas kernels, local(): pl.pallas_call(kernel, out_shape=(pltpu.VMEM(trace, F32), pltpu.VMEM((RHS...  73.4 us

profile of v5, /device:TPU:1, one launch (start us, length us, event | category | flops | bytes accessed | tf_op | source)
XLA Modules:
  0.0 74.7 jit_solution(14470693015559505657)
XLA Ops:
  0.6 73.4 %sweep.1 = (f32[2,32,1024]{2,1,0:T(8,128)S(1)}, f32[32,256]{1,0:T(8,128)S(1)}) custom-call(f32[2,32,1024]{2,1,0:T(8,128)} %bitcast.15, f32[32,256]{1,0:T(8,128)} %bitcast.16, bf16[2,1024,1024]{2,1,0:T(8,128)(2,1)} %bitcast.11, bf16[2,1024,512]{2,1,0:T(8,128)(2,1)} %bitcast.12, bf16[2,16,2,16,1024]{4,3,2,1,0:T(8,128)(2,1)} %bitcast.13, ...), custom_call_target="tpu_custom_call" | custom-call | tf_op jit(solution)/shard_map/sweep/pallas_call | solution.py:592
  74.0 0.7 hand_over.1

commit v6 on v5

--- a/solution.py
+++ b/solution.py
@@ -38,7 +38,7 @@
     leaf_out, sep_out,
     A, PP, QQ, LL, LW, SS, SL, CP, CT,
     T, U, TS, US, DA, E, DB, G, UA, UB,
-    Z, ZP, PMS, PMR, UPS, UPR, ONE, RED, PKS, PKR,
+    NL, QL, DL, GL, Z, ZP, PMS, PMR, UPS, UPR, ONE, RED, PKS, PKR,
     lsem, ps, pr, dsnd, drcv, usnd, urcv, osnd, orcv, rsnd, rrcv,
 ):
     p = lax.axis_index("panel")
@@ -502,27 +502,22 @@
 
             lax.fori_loop(0, 2, before, 0)
 
+            for f in range(2):
+                ship_q[f].wait_recv()
+
             def ready(f, g):
-                @pl.when(g == 0)
-                def _():
-                    to_pair(QQ.at[f], QQ.at[f], S_Q + f).wait_recv()
-
                 up_wave(f, g).wait_recv()
 
             def left_of(f, rows):
                 return U[f, rows, :]
 
-            @pl.when(first)
-            def _():
-                waves(ready, left_of, QQ, G, UA, US, None)
-
             @pl.when(c > 0)
             def _():
                 waves(ready, left_of, QQ, G, UA, US, send_up)
 
-        def lifted(x, half):
+        def lifted(x, update_of):
             for f in range(2):
-                Z[f * RHS : (f + 1) * RHS, :] = dot(half[f], LL[x, f])
+                Z[f * RHS : (f + 1) * RHS, :] = update_of(f)
             rows = Z[0 : 2 * RHS, :].T.reshape(PEERS, 2, ROWS, 2 * RHS)
             packed = jnp.concatenate([rows[:, 0], rows[:, 1]], axis=-1)
             UPS[x] = packed.reshape(SHARE, 128).astype(BF16)
@@ -530,29 +525,62 @@
 
         send_lift.wait_recv()
         own_lift.wait()
-        lifted(0, US)
-        ship_ua.start()
-
-        @pl.when(last)
-        def _():
-            def rest(f, _):
-                UB[f] = DB[f] + dot(T[f], PP[f])
+
+        def own_rest(f, _):
+            loaded = coupled(1, f, 2) * U[f].astype(F32)
+            UB[f] = DB[f] + dot(loaded.astype(BF16), A[1, f])
+            return 0
+
+        @pl.when(first)
+        def _():
+            CT[1] = CP[1].T
+            for f in range(2):
+
+                @pl.loop(0, 4)
+                def _(b):
+                    rows = pl.ds(pl.multiple_of(b * 256, 256), 256)
+                    QL[f, rows, :] = dot(QQ[f, rows, :], LL[0, f]).astype(BF16)
+                    both = dot(A[1, f, rows, :], LL[1, f]) * CT[1, rows, f + 2 : f + 3]
+                    NL[f, rows, :] = both.astype(BF16)
+
+                GL[f] = dot(G[f].astype(BF16), LL[0, f])
+                DL[f] = dot(DB[f].astype(BF16), LL[1, f])
+
+            def from_wave(f):
+                for g in range(2):
+                    up_wave(f, g).wait_recv()
+                return GL[f] + dot(U[f], QL[f])
+
+            lifted(0, from_wave)
+            lifted(1, lambda f: DL[f] + dot(U[f], NL[f]))
+
+            def last_solve(f, _):
+                UA[f] = G[f] + dot(U[f], QQ[f])
                 return 0
 
-            lax.fori_loop(0, 2, rest, 0)
-
-        @pl.when(c < LAST)
-        def _():
-            def rest(f, _):
-                loaded = coupled(1, f, 2) * U[f].astype(F32)
-                UB[f] = DB[f] + dot(loaded.astype(BF16), A[1, f])
-                return 0
-
-            lax.fori_loop(0, 2, rest, 0)
-
-        for f in range(2):
-            DA[f] = UB[f].astype(BF16)
-        lifted(1, DA)
+            lax.fori_loop(0, 2, last_solve, 0)
+            ship_ua.start()
+            lax.fori_loop(0, 2, own_rest, 0)
+
+        @pl.when(c > 0)
+        def _():
+            lifted(0, lambda f: dot(US[f], LL[0, f]))
+            ship_ua.start()
+
+            @pl.when(last)
+            def _():
+                def rest(f, _):
+                    UB[f] = DB[f] + dot(T[f], PP[f])
+                    return 0
+
+                lax.fori_loop(0, 2, rest, 0)
+
+            @pl.when(c < LAST)
+            def _():
+                lax.fori_loop(0, 2, own_rest, 0)
+
+            lifted(1, lambda f: dot(UB[f].astype(BF16), LL[1, f]))
+
         separator(1, UB)
 
         for copy in (send_cp, *send_a, ship_ua):
@@ -606,6 +634,8 @@
             pltpu.VMEM((2, LEAF, 8), F32),
             *[pltpu.VMEM(trace, BF16) for _ in range(5)],
             *[pltpu.VMEM(trace, F32) for _ in range(5)],
+            *[pltpu.VMEM((2, LEAF, UPD), BF16) for _ in range(2)],
+            *[pltpu.VMEM((2, RHS, UPD), F32) for _ in range(2)],
             pltpu.VMEM((128, UPD), F32),
             pltpu.VMEM((128, SHARE), F32),
             pltpu.VMEM((SHARE, 128), F32),

time: 74.8 us -> 73.9 us (0.988)
  Pallas kernels: 74.1 us -> 73.2 us
    pallas_call x1, Pallas kernels: 73.4 us -> 72.4 us  [local(): pl.pallas_call(kernel, out_shape=(pltpu.VMEM(trace, F32), pltpu.VMEM((RHS...]
where the time goes in v6:
time: 73.9 us; the launch traced here: 73.8 us
  Pallas kernels  73.2 us (99%)
    pallas_call x1, Pallas kernels, local(): pl.pallas_call(kernel, out_shape=(pltpu.VMEM(trace, F32), pltpu.VMEM((RHS...  72.4 us

profile of v6, /device:TPU:1, one launch (start us, length us, event | category | flops | bytes accessed | tf_op | source)
XLA Modules:
  0.0 73.8 jit_solution(15284359371571605536)
XLA Ops:
  0.6 72.4 %sweep.1 = (f32[2,32,1024]{2,1,0:T(8,128)S(1)}, f32[32,256]{1,0:T(8,128)S(1)}) custom-call(f32[2,32,1024]{2,1,0:T(8,128)} %bitcast.15, f32[32,256]{1,0:T(8,128)} %bitcast.16, bf16[2,1024,1024]{2,1,0:T(8,128)(2,1)} %bitcast.11, bf16[2,1024,512]{2,1,0:T(8,128)(2,1)} %bitcast.12, bf16[2,16,2,16,1024]{4,3,2,1,0:T(8,128)(2,1)} %bitcast.13, ...), custom_call_target="tpu_custom_call" | custom-call | tf_op jit(solution)/shard_map/sweep/pallas_call | solution.py:620
  73.1 0.7 hand_over.1

commit v7 on v6

--- a/solution.py
+++ b/solution.py
@@ -320,7 +320,14 @@
     @pl.when(is1)
     def _core1():
         send_cp.start()
-        give_a()
+        for copy in own:
+            copy.wait()
+
+        @pl.when(c > DIRECT)
+        def _():
+            give_front(0)
+            give_front(1)
+
         send_targets()
         own_sep.start()
         own_lift.start()
@@ -444,6 +451,8 @@
 
         @pl.when(c <= DIRECT)
         def _():
+            give_front(0)
+            give_front(1)
             build_maps()
 
         @pl.when(c > DIRECT)

time: 73.9 us -> 73.9 us (level)
  no operation moved by 1% of the time
where the time goes in v7:
time: 73.9 us; the launch traced here: 73.8 us
  Pallas kernels  73.2 us (99%)
    pallas_call x1, Pallas kernels, local(): pl.pallas_call(kernel, out_shape=(pltpu.VMEM(trace, F32), pltpu.VMEM((RHS...  72.4 us

profile of v7, /device:TPU:1, one launch (start us, length us, event | category | flops | bytes accessed | tf_op | source)
XLA Modules:
  0.0 73.8 jit_solution(4063021041333050570)
XLA Ops:
  0.6 72.4 %sweep.1 = (f32[2,32,1024]{2,1,0:T(8,128)S(1)}, f32[32,256]{1,0:T(8,128)S(1)}) custom-call(f32[2,32,1024]{2,1,0:T(8,128)} %bitcast.15, f32[32,256]{1,0:T(8,128)} %bitcast.16, bf16[2,1024,1024]{2,1,0:T(8,128)(2,1)} %bitcast.11, bf16[2,1024,512]{2,1,0:T(8,128)(2,1)} %bitcast.12, bf16[2,16,2,16,1024]{4,3,2,1,0:T(8,128)(2,1)} %bitcast.13, ...), custom_call_target="tpu_custom_call" | custom-call | tf_op jit(solution)/shard_map/sweep/pallas_call | solution.py:629
  73.1 0.7 hand_over.1
